TPU v7x, 256 devices: a whole 4x4x8 slice. The times are simulated.
256 devices in a mesh: lat: 8 (over y_hi, x), lon: 32 (over y_lo, z, core).
Axes of the slice: x: 4, y: 4 (y_hi: 2, y_lo: 2; y = y_hi * 2 + y_lo), z: 8, core: 2. Of those that a mesh axis runs over, the one named last changes fastest.
Arguments:
- queries: bfloat16 [64, 512, 1024], P('lat', 'lon'), may hold values from -180 to 180
- keys: bfloat16 [64, 512, 1024], P('lat', 'lon'), may hold values from -6 to 6
- values: bfloat16 [64, 512, 1024], P('lat', 'lon'), may hold values from -6 to 6
- cotangent: bfloat16 [64, 512, 1024], P('lat', 'lon'), may hold values from -6 to 6
- near_pattern: int32 [16, 13, 13], replicated, may hold values 0 or 1
- zonal_pattern: int32 [64, 32], P('lat'), may hold values 0 or 1
Outputs:
- attended: bfloat16 [64, 512, 1024], P('lat', 'lon')
- grad_queries: bfloat16 [64, 512, 1024], P('lat', 'lon')
- grad_keys: bfloat16 [64, 512, 1024], P('lat', 'lon')
- grad_values: bfloat16 [64, 512, 1024], P('lat', 'lon')
All inputs are finite; a program needn't handle non-finite values. No bound on the sum of `zonal_pattern` on one device may be relied on, other than what follows from the above.
Results may differ from a plain program's by a relative error of at most 0.014.
Values may be sent and summed in bfloat16 or wider, within the bound.
A program may use at most 128 MiB of HBM per device.

v0:
```python
import jax
import jax.numpy as jnp
import numpy as np
from jax import lax
from jax.sharding import PartitionSpec as P

RADIUS = 6


def with_halo(cells, sides, width, closed):
    for axis, dim in sides:
        count = lax.axis_size(axis)
        ends = count if closed else count - 1
        head = lax.slice_in_dim(cells, 0, width, axis=dim)
        tail = lax.slice_in_dim(cells, cells.shape[dim] - width, cells.shape[dim], axis=dim)
        cells = jnp.concatenate(
            [
                lax.ppermute(tail, axis, [(i, (i + 1) % count) for i in range(ends)]),
                cells,
                lax.ppermute(head, axis, [((i + 1) % count, i) for i in range(ends)]),
            ],
            axis=dim,
        )
    return cells


def offset_selectors(tile_rows, tile_cols):
    window_span = 2 * RADIUS + 1
    query_rows = np.arange(tile_rows)[:, None, None]
    region_rows = np.arange(tile_rows + 2 * RADIUS)[None, :, None]
    offsets = np.arange(window_span)[None, None, :]
    row_select = (region_rows - query_rows == offsets).astype(np.float32)
    query_cols = np.arange(tile_cols)[:, None, None]
    region_cols = np.arange(tile_cols + 2 * RADIUS)[None, :, None]
    col_select = (region_cols - query_cols == offsets).astype(np.float32)
    return (row_select, col_select)


def near_allowed(near_pattern):
    window_span = 2 * RADIUS + 1
    centre = (jnp.arange(window_span)[:, None] == RADIUS) & (
        jnp.arange(window_span)[None, :] == RADIUS
    )
    return ((near_pattern == 1) | centre[None]).astype(jnp.float32)


def window_mask(pattern_float, row_select, col_select, rows_ok):
    head_count = pattern_float.shape[0]
    row_part = jnp.asarray(row_select) * rows_ok.astype(jnp.float32)[None, :, None]
    partial_rows = jnp.einsum(
        "hab,rka->hrkb", pattern_float, row_part, precision=lax.Precision.HIGHEST
    )
    full = jnp.einsum(
        "hrkb,cjb->hrckj", partial_rows, jnp.asarray(col_select), precision=lax.Precision.HIGHEST
    )
    count_q = row_select.shape[0] * col_select.shape[0]
    count_k = row_select.shape[1] * col_select.shape[1]
    return full.reshape(head_count, count_q, count_k) > 0.5


def split_rims(gradients, dimension):
    length = gradients.shape[dimension]
    low_rim = lax.slice_in_dim(gradients, 0, RADIUS, axis=dimension)
    high_rim = lax.slice_in_dim(gradients, length - RADIUS, length, axis=dimension)
    return jnp.concatenate([low_rim, high_rim], axis=dimension)


def fold_rims(gradients, arrived, dimension):
    interior = lax.slice_in_dim(
        gradients, RADIUS, gradients.shape[dimension] - RADIUS, axis=dimension
    )
    length = interior.shape[dimension]
    front_rim = lax.slice_in_dim(arrived, 0, RADIUS, axis=dimension)
    back_rim = lax.slice_in_dim(
        arrived, arrived.shape[dimension] - RADIUS, arrived.shape[dimension], axis=dimension
    )
    front_pad = [(0, 0)] * gradients.ndim
    back_pad = [(0, 0)] * gradients.ndim
    front_pad[dimension] = (0, length - RADIUS)
    back_pad[dimension] = (length - RADIUS, 0)
    return interior + jnp.pad(front_rim, front_pad) + jnp.pad(back_rim, back_pad)


def body(queries, keys, values, cotangent, near_pattern, zonal_pattern):
    band_rows, band_cols, features = queries.shape
    head_count = near_pattern.shape[0]
    head_size = features // head_count
    softmax_scale = head_size ** (-0.5)
    tile_rows = 8
    tile_cols = min(band_cols, 32)
    region_rows = tile_rows + 2 * RADIUS
    region_cols = tile_cols + 2 * RADIUS
    count_q = tile_rows * tile_cols
    count_k = region_rows * region_cols
    row_select, col_select = offset_selectors(tile_rows, tile_cols)
    pattern_float = near_allowed(near_pattern)
    ext_rows = jnp.arange(band_rows + 2 * RADIUS) + lax.axis_index("lat") * band_rows - RADIUS
    row_valid = (ext_rows >= 0) & (ext_rows < band_rows * lax.axis_size("lat"))
    masks = {}
    row_start = 0
    masks[row_start] = window_mask(pattern_float, row_select, col_select, row_valid)
    stacked = jnp.stack([keys, values])
    widened = with_halo(stacked, (("lon", 2),), RADIUS, True)
    region = with_halo(widened, (("lat", 1),), RADIUS, False)
    pooled = (jnp.sum(stacked, axis=2, dtype=jnp.float32) * band_cols ** (-0.5)).astype(
        jnp.bfloat16
    )[:, :, None, :]
    zonal_ok = zonal_pattern == 1
    query_heads = queries.reshape(band_rows, band_cols, head_count, head_size)
    grad_heads = cotangent.reshape(band_rows, band_cols, head_count, head_size)
    gathered = lax.all_gather(pooled, "lon", axis=2, tiled=True)
    running_max = jnp.full((head_count, band_rows, band_cols), -1e30, jnp.float32)
    amount = gathered.shape[2]
    sector_ok = zonal_ok[None, :, None, :]
    sector_keys = gathered[0].reshape(band_rows, amount, head_count, head_size)
    sector_values = (
        gathered[1].reshape(band_rows, amount, head_count, head_size).astype(jnp.float32)
    )
    scores = (
        jnp.einsum("rchd,rshd->hrcs", query_heads, sector_keys, preferred_element_type=jnp.float32)
        * softmax_scale
    )
    new_max = jnp.maximum(running_max, jnp.max(jnp.where(sector_ok, scores, -1e30), axis=3))
    weight = jnp.where(sector_ok, jnp.exp(scores - new_max[..., None]), 0.0)
    running_sum = jnp.sum(weight, axis=3)
    running_acc = jnp.einsum(
        "hrcs,rshd->rchd", weight, sector_values, precision=lax.Precision.HIGHEST
    )
    tile_list = [
        (row_start, col_start)
        for row_start in range(0, band_rows, tile_rows)
        for col_start in range(0, band_cols, tile_cols)
    ]

    def tile_parts(row_start):
        kv_block = region.reshape(2, count_k, head_count, head_size)
        query_tile = queries.reshape(count_q, head_count, head_size)
        admitted = masks[row_start]
        scores = (
            jnp.einsum("qhd,khd->hqk", query_tile, kv_block[0], preferred_element_type=jnp.float32)
            * softmax_scale
        )
        return (kv_block, query_tile, admitted, scores)

    def heads_tile(grid):
        return grid.reshape(head_count, count_q)

    outputs = jnp.zeros((band_rows, band_cols, features), jnp.float32)
    lse_grid = jnp.zeros((head_count, band_rows, band_cols), jnp.float32)
    row_start, col_start = tile_list[0]
    kv_block, query_tile, admitted, scores = tile_parts(row_start)
    tile_zonal_max = heads_tile(new_max)
    tile_zonal_total = heads_tile(running_sum)
    tile_zonal_acc = running_acc.reshape(count_q, head_count, head_size)
    highest_score = jnp.maximum(jnp.max(jnp.where(admitted, scores, -1e30), axis=2), tile_zonal_max)
    denominator = jnp.sum(
        jnp.where(admitted, jnp.exp(scores - highest_score[..., None]), 0.0), axis=2
    ) + tile_zonal_total * jnp.exp(tile_zonal_max - highest_score)
    tile_lse = highest_score + jnp.log(denominator)
    near_weights = jnp.where(admitted, jnp.exp(scores - tile_lse[..., None]), 0.0).astype(
        jnp.bfloat16
    )
    tile_output = jnp.einsum(
        "hqk,khd->qhd", near_weights, kv_block[1], preferred_element_type=jnp.float32
    )
    tile_output = tile_output + tile_zonal_acc * jnp.exp(tile_zonal_max - tile_lse).T[..., None]
    outputs = outputs.at[row_start : row_start + tile_rows, col_start : col_start + tile_cols].set(
        tile_output.reshape(tile_rows, tile_cols, features)
    )
    lse_grid = lse_grid.at[
        :, row_start : row_start + tile_rows, col_start : col_start + tile_cols
    ].set(tile_lse.reshape(head_count, tile_rows, tile_cols))
    attended = outputs.astype(jnp.bfloat16)
    deltas = jnp.transpose(
        jnp.sum(grad_heads * outputs.reshape(band_rows, band_cols, head_count, head_size), axis=3),
        (2, 0, 1),
    )
    gradients = jnp.zeros(
        (2, band_rows + 2 * RADIUS, band_cols + 2 * RADIUS, features), jnp.float32
    )
    near_query_grad = jnp.zeros((band_rows, band_cols, features), jnp.float32)
    row_start, col_start = tile_list[0]
    kv_block, query_tile, admitted, scores = tile_parts(row_start)
    tile_lse = heads_tile(lse_grid)
    tile_deltas = heads_tile(deltas)
    grad_tile = cotangent.reshape(count_q, head_count, head_size)
    weights = jnp.where(admitted, jnp.exp(scores - tile_lse[..., None]), 0.0)
    grad_weights = jnp.einsum(
        "qhd,khd->hqk", grad_tile, kv_block[1], preferred_element_type=jnp.float32
    )
    grad_scores = (weights * (grad_weights - tile_deltas[..., None]) * softmax_scale).astype(
        jnp.bfloat16
    )
    query_grad = jnp.einsum(
        "hqk,khd->qhd", grad_scores, kv_block[0], preferred_element_type=jnp.float32
    )
    key_grad = jnp.einsum(
        "hqk,qhd->khd", grad_scores, query_tile, preferred_element_type=jnp.float32
    )
    value_grad = jnp.einsum(
        "hqk,qhd->khd", weights.astype(jnp.bfloat16), grad_tile, preferred_element_type=jnp.float32
    )
    section = jnp.stack([key_grad, value_grad]).reshape(2, region_rows, region_cols, features)
    gradients = gradients.at[
        :, row_start : row_start + region_rows, col_start : col_start + region_cols
    ].add(section)
    near_query_grad = near_query_grad.at[
        row_start : row_start + tile_rows, col_start : col_start + tile_cols
    ].set(query_grad.reshape(tile_rows, tile_cols, features))
    amount = gathered.shape[2]
    sector_ok = zonal_ok[None, :, None, :]
    sector_keys = gathered[0].reshape(band_rows, amount, head_count, head_size)
    sector_values = gathered[1].reshape(band_rows, amount, head_count, head_size)
    scores = (
        jnp.einsum("rchd,rshd->hrcs", query_heads, sector_keys, preferred_element_type=jnp.float32)
        * softmax_scale
    )
    weights = jnp.where(sector_ok, jnp.exp(scores - lse_grid[..., None]), 0.0)
    grad_weights = jnp.einsum(
        "rchd,rshd->hrcs", grad_heads, sector_values, preferred_element_type=jnp.float32
    )
    grad_scores = (weights * (grad_weights - deltas[..., None]) * softmax_scale).astype(
        jnp.bfloat16
    )
    query_acc = jnp.einsum(
        "hrcs,rshd->rchd", grad_scores, sector_keys, preferred_element_type=jnp.float32
    )
    key_part = jnp.einsum(
        "hrcs,rchd->srhd", grad_scores, query_heads, preferred_element_type=jnp.float32
    )
    value_part = jnp.einsum(
        "hrcs,rchd->srhd",
        weights.astype(jnp.bfloat16),
        grad_heads,
        preferred_element_type=jnp.float32,
    )
    section = jnp.stack([key_part, value_part], axis=1).reshape(amount, 2, band_rows, features)
    partials = section
    zonal_query_grad, partials = (query_acc, partials)
    owned_grad = lax.psum_scatter(
        partials.astype(jnp.bfloat16), "lon", scatter_dimension=0, tiled=True
    ).astype(jnp.float32)[0]
    arrived = with_halo(split_rims(gradients, 1), (("lat", 1),), RADIUS, False)
    gradients = fold_rims(gradients, arrived, 1)
    arrived = with_halo(
        split_rims(gradients, 2).astype(jnp.bfloat16), (("lon", 2),), RADIUS, True
    ).astype(jnp.float32)
    gradients = fold_rims(gradients, arrived, 2)
    kv_grads = gradients + owned_grad[:, :, None, :] * band_cols ** (-0.5)
    query_total = near_query_grad + zonal_query_grad.reshape(band_rows, band_cols, features)
    return (
        attended,
        query_total.astype(jnp.bfloat16),
        kv_grads[0].astype(jnp.bfloat16),
        kv_grads[1].astype(jnp.bfloat16),
    )


def solution(mesh):
    placed = (
        P("lat", "lon", None),
        P("lat", "lon", None),
        P("lat", "lon", None),
        P("lat", "lon", None),
        P(),
        P("lat", None),
    )
    return jax.shard_map(
        body,
        mesh=mesh,
        in_specs=placed,
        out_specs=(
            P("lat", "lon", None),
            P("lat", "lon", None),
            P("lat", "lon", None),
            P("lat", "lon", None),
        ),
        check_vma=False,
    )
```

profile of v0, /device:TPU:1, one launch (start us, length us, event | category | flops | bytes accessed | tf_op | source)
XLA Modules:
  0.0 424.6 jit_solution(2678378158538720729)
XLA Ops:
  10.4 3.3 collective-permute-start.1
  24.5 5.1 %collective-permute-start.2 = (bf16[2,6,28,1024]{3,0,2,1:T(2,128)(2,1)}, bf16[2,6,28,1024]{3,0,2,1:T(2,128)(2,1)}, u32[]{:S(2)}, u32[]{:S(2)}) collective-permute-start(bf16[2,6,28,1024]{3,0,2,1:T(2,128)(2,1)} %copy.106), channel_id=1, source_target_pairs={{0,32},{32,64},{64,96},{96,128},{128,160},{160,192},{192,224},{1,3... | collective-permute-start | bytes 2064392 | tf_op jit(solution)/shard_map/ppermute | solution.py:18
  29.7 24.2 %compare_bitcast_fusion = pred[16,8,16,20,28]{4,3,2,1,0:T(8,128)(4,1)} fusion(f32[16,8,20,13,1]{2,3,4,1,0:T(8,128)S(1)} %convolution_bitcast_fusion.3, f32[16,28,13,1,1]{1,2,0,4,3:T(8,128)S(1)} %copy-done.30), kind=kOutput, calls=%fused_computation | convolution fusion | flops 180060160 | bytes 1303296 | tf_op jit(solution)/shard_map/hrkb,cjb->hrckj/dot_general | solution.py:53
  58.8 12.5 %gt.15 = pred[16,128,560]{2,1,0:T(8,128)(4,1)S(1)} reshape(pred[16,8,16,20,28]{4,3,2,1,0:T(8,128)(4,1)} %compare_bitcast_fusion) | data formatting | bytes 2293760 | tf_op jit(solution)/shard_map/gt | solution.py:58
  71.3 2.3 copy.117
  81.7 3.2 squeeze.5
  84.9 3.7 copy.111
  88.6 3.2 squeeze.4
  91.9 3.9 copy.118
  95.8 4.6 %fusion.2 = (f32[16,128]{1,0:T(8,128)S(1)}, f32[16,560,128]{2,1,0:T(8,128)}) fusion(pred[16,128,560]{1,2,0:T(8,128)(4,1)S(1)} %copy.117, bf16[560,16,64]{0,2,1:T(8,128)(2,1)} %copy.111, bf16[128,16,64]{0,2,1:T(8,128)(2,1)} %copy.112), kind=kOutput, calls=%fused_computation.8 | convolution fusion | flops 150239232 | bytes 7151616 | tf_op jit(solution)/shard_map/qhd,khd->hqk/dot_general | solution.py:140
  110.0 2.7 convolution_bitcast_fusion.2
  115.7 3.6 fusion.5
  120.1 5.2 %convolution_bitcast_fusion = f32[560,16,64]{0,2,1:T(8,128)} fusion(bf16[128,16,64]{0,2,1:T(8,128)(2,1)} %copy.125, pred[16,128,560]{1,2,0:T(8,128)(4,1)S(1)} %copy.117, f32[16,560,128]{2,1,0:T(8,128)} %get-tuple-element.113, f32[16,128]{1,0:T(8,128)S(1)} %get-tuple-element.91), kind=kOutput, calls=%fused_computation.18 | convolution fusion | flops 151388160 | bytes 8298496 | tf_op jit(solution)/shard_map/hqk,qhd->khd/dot_general | solution.py:200
  127.6 4.9 %fusion.1 = bf16[16,128,560]{1,2,0:T(8,128)(2,1)S(1)} fusion(pred[16,128,560]{1,2,0:T(8,128)(4,1)S(1)} %copy.117, f32[16,560,128]{2,1,0:T(8,128)} %get-tuple-element.113, f32[16,128]{1,0:T(8,128)S(1)} %sub.91, f32[16,128]{1,0:T(8,128)S(1)} %get-tuple-element.91, bf16[560,16,64]{0,2,1:T(8,128)(2,1)S(1)} %copy-done.15, bf16[128,16,64]{0,2,1:T(8,128)(2,1)} %copy.125), kind=kOutput, calls=%fused_computation.4 | convolution fusion | flops 154828800 | bytes 9453568 | tf_op jit(solution)/shard_map/qhd,khd->hqk/dot_general | solution.py:188
  133.5 2.5 convolution_bitcast_fusion.1
  136.0 4.6 %copy.137 = f32[560,16,64]{2,1,0:T(8,128)} copy(f32[560,16,64]{0,2,1:T(8,128)S(1)} %copy-done.10) | data formatting | bytes 4587520 | tf_op jit(solution)/shard_map/hqk,qhd->khd/transpose | solution.py:200
  140.7 3.7 stack.31
  144.4 5.7 %copy.135 = f32[560,16,64]{2,1,0:T(8,128)} copy(f32[560,16,64]{0,2,1:T(8,128)} %convolution_bitcast_fusion.1) | data formatting | bytes 4587520 | tf_op jit(solution)/shard_map/hqk,qhd->khd/transpose | solution.py:197
  150.1 5.0 %stack.30 = f32[1,1,20,28,1024]{4,3,2,1,0:T(8,128)} reshape(f32[560,16,64]{2,1,0:T(8,128)} %copy.135) | data formatting | bytes 4587520 | tf_op jit(solution)/shard_map/stack | solution.py:203
  155.2 2.3 maximum_bitcast_fusion
  165.5 5.2 %collective-permute-start.4 = (f32[2,6,28,1024]{3,0,2,1:T(2,128)}, f32[2,6,28,1024]{3,0,2,1:T(2,128)}, u32[]{:S(2)}, u32[]{:S(2)}) collective-permute-start(f32[2,6,28,1024]{3,0,2,1:T(2,128)} %copy.138), channel_id=1, source_target_pairs={{0,32},{32,64},{64,96},{96,128},{128,160},{160,192},{192,224},{1,3... | collective-permute-start | bytes 4128776 | tf_op jit(solution)/shard_map/ppermute | solution.py:18
  183.2 5.2 %collective-permute-done.5 = f32[2,6,28,1024]{3,0,2,1:T(2,128)} collective-permute-done((f32[2,6,28,1024]{3,0,2,1:T(2,128)}, f32[2,6,28,1024]{3,0,2,1:T(2,128)}, u32[]{:S(2)}, u32[]{:S(2)}) %collective-permute-start.5) | collective-permute-done | bytes 1376288 | tf_op jit(solution)/shard_map/ppermute | solution.py:20
  195.8 8.7 %collective-permute-start.7 = (bf16[2,8,6,1024]{3,2,1,0:T(8,128)(2,1)S(1)}, bf16[2,8,6,1024]{3,2,1,0:T(8,128)(2,1)S(1)}, u32[]{:S(2)}, u32[]{:S(2)}) collective-permute-start(bf16[2,8,6,1024]{3,2,1,0:T(8,128)(2,1)S(1)} %get-tuple-element.99), channel_id=1, source_target_pairs={{1,0},{2,1},{3,2},{4,3},{5,4},{6,5},{7,6},{8,7},{9,8},{10,9},{11,1... | collective-permute-start | bytes 589832 | tf_op jit(solution)/shard_map/ppermute | solution.py:20
  207.7 205.7 %all-reduce.6.cloned.1.call-done = bf16[32,2,8,1024]{3,2,0,1:T(8,128)(2,1)} async-done(((bf16[32,2,8,1024]{3,2,0,1:T(8,128)(2,1)}), bf16[32,2,8,1024]{3,2,0,1:T(8,128)(2,1)}) %all-reduce.6.cloned.1.call-update) | async-done | bytes 1048592
  (156 shorter events, 78.4 us)
Async XLA Ops:
  7.2 12.1 %copy-start.8 = (bf16[8,16,1024]{2,1,0:T(8,128)(2,1)S(1)}, bf16[8,16,1024]{2,1,0:T(8,128)(2,1)}, u32[]{:S(2)}) copy-start(bf16[8,16,1024]{2,1,0:T(8,128)(2,1)} %param.26) | copy-start | bytes 786436
  7.2 12.1 %copy-start.9 = (bf16[8,16,1024]{2,1,0:T(8,128)(2,1)S(1)}, bf16[8,16,1024]{2,1,0:T(8,128)(2,1)}, u32[]{:S(2)}) copy-start(bf16[8,16,1024]{2,1,0:T(8,128)(2,1)} %param.25) | copy-start | bytes 786436
  7.2 93.9 %all-gather.3.cloned.1.call-start = ((), (), s32[]{:S(2)}) async-start(), calls=%async_computation | async-start | bytes 1081344 | tf_op jit(solution)/shard_map/all_gather | solution.py:111
  9.1 404.3 %all-reduce.6.cloned.1.call-start = ((), (), s32[]{:S(2)}) async-start(), calls=%async_computation.1 | async-start | bytes 2097152
  10.4 7.2 %collective-permute-start.1 = (bf16[2,8,6,1024]{3,2,1,0:T(8,128)(2,1)S(1)}, bf16[2,8,6,1024]{3,2,1,0:T(8,128)(2,1)S(1)}, u32[]{:S(2)}, u32[]{:S(2)}) collective-permute-start(bf16[2,8,6,1024]{3,2,1,0:T(8,128)(2,1)S(1)} %get-tuple-element.109), channel_id=1, source_target_pairs={{1,0},{2,1},{3,2},{4,3},{5,4},{6,5},{7,6},{8,7},{9,8},{10,9},{11,1... | collective-permute-start | bytes 589832 | tf_op jit(solution)/shard_map/ppermute | solution.py:20
  13.7 5.6 %collective-permute-start = (bf16[2,8,6,1024]{3,2,1,0:T(8,128)(2,1)S(1)}, bf16[2,8,6,1024]{3,2,1,0:T(8,128)(2,1)S(1)}, u32[]{:S(2)}, u32[]{:S(2)}) collective-permute-start(bf16[2,8,6,1024]{3,2,1,0:T(8,128)(2,1)S(1)} %get-tuple-element.108), channel_id=1, source_target_pairs={{0,1},{1,2},{2,3},{3,4},{4,5},{5,6},{6,7},{7,8},{8,9},{9,10},{10,1... | collective-permute-start | bytes 589832 | tf_op jit(solution)/shard_map/ppermute | solution.py:18
  19.8 9.8 %copy-start.30 = (f32[16,28,13,1,1]{1,2,0,4,3:T(8,128)S(1)}, f32[16,28,13,1,1]{1,2,0,4,3:T(8,128)}, u32[]{:S(2)}) copy-start(f32[16,28,13,1,1]{1,2,0,4,3:T(8,128)} %constant.191) | copy-start | bytes 69892
  21.6 54.9 %collective-permute-start.3 = (bf16[2,6,28,1024]{3,0,2,1:T(2,128)(2,1)}, bf16[2,6,28,1024]{3,0,2,1:T(2,128)(2,1)}, u32[]{:S(2)}, u32[]{:S(2)}) collective-permute-start(bf16[2,6,28,1024]{3,0,2,1:T(2,128)(2,1)} %copy.107), channel_id=1, source_target_pairs={{32,0},{64,32},{96,64},{128,96},{160,128},{192,160},{224,192},{33,... | collective-permute-start | bytes 2064392 | tf_op jit(solution)/shard_map/ppermute | solution.py:20
  24.5 29.4 %copy-start.16 = (bf16[8,16,1024]{2,1,0:T(8,128)(2,1)S(1)}, bf16[8,16,1024]{2,1,0:T(8,128)(2,1)}, u32[]{:S(2)}) copy-start(bf16[8,16,1024]{2,1,0:T(8,128)(2,1)} %param.24) | copy-start | bytes 786436
  24.5 31.7 %copy-start.17 = (bf16[8,16,1024]{2,1,0:T(8,128)(2,1)S(1)}, bf16[8,16,1024]{2,1,0:T(8,128)(2,1)}, u32[]{:S(2)}) copy-start(bf16[8,16,1024]{2,1,0:T(8,128)(2,1)} %param.27) | copy-start | bytes 786436
  24.5 53.3 %collective-permute-start.2 = (bf16[2,6,28,1024]{3,0,2,1:T(2,128)(2,1)}, bf16[2,6,28,1024]{3,0,2,1:T(2,128)(2,1)}, u32[]{:S(2)}, u32[]{:S(2)}) collective-permute-start(bf16[2,6,28,1024]{3,0,2,1:T(2,128)(2,1)} %copy.106), channel_id=1, source_target_pairs={{0,32},{32,64},{64,96},{96,128},{128,160},{160,192},{192,224},{1,3... | collective-permute-start | bytes 2064392 | tf_op jit(solution)/shard_map/ppermute | solution.py:18
  106.5 6.2 %copy-start.2 = (f32[16,8,32,16]{2,3,1,0:T(8,128)}, f32[16,8,32,16]{2,3,1,0:T(8,128)S(1)}, u32[]{:S(2)}) copy-start(f32[16,8,32,16]{2,3,1,0:T(8,128)S(1)} %get-tuple-element.111) | copy-start | bytes 786436
  115.7 9.6 %slice-start = ((s8[4587520]{0:T(1024)(128)(4,1)}), s8[393216]{0:T(1024)(128)(4,1)S(1)}, s32[]{:S(2)}) async-start(s8[4587520]{0:T(1024)(128)(4,1)} %bitcast.101), calls=%async_computation.2 | async-start | bytes 786432
  159.8 10.9 %copy-start.22 = (f32[16,8,16]{2,1,0:T(8,128)S(1)}, f32[16,8,16]{2,1,0:T(8,128)}, u32[]{:S(2)}) copy-start(f32[16,8,16]{2,1,0:T(8,128)} %reduce_max.22) | copy-start | bytes 24580
  159.8 11.0 %copy-start.24 = (f32[16,8,16]{2,1,0:T(8,128)S(1)}, f32[16,8,16]{2,1,0:T(8,128)}, u32[]{:S(2)}) copy-start(f32[16,8,16]{2,1,0:T(8,128)} %copy-done.23) | copy-start | bytes 24580
  159.8 11.0 %copy-start.25 = (f32[16,8,16]{2,1,0:T(8,128)S(1)}, f32[16,8,16]{2,1,0:T(8,128)}, u32[]{:S(2)}) copy-start(f32[16,8,16]{2,1,0:T(8,128)} %reduce_sum.45) | copy-start | bytes 24580
  162.0 26.4 %collective-permute-start.5 = (f32[2,6,28,1024]{3,0,2,1:T(2,128)}, f32[2,6,28,1024]{3,0,2,1:T(2,128)}, u32[]{:S(2)}, u32[]{:S(2)}) collective-permute-start(f32[2,6,28,1024]{3,0,2,1:T(2,128)} %copy.140), channel_id=1, source_target_pairs={{32,0},{64,32},{96,64},{128,96},{160,128},{192,160},{224,192},{33,... | collective-permute-start | bytes 4128776 | tf_op jit(solution)/shard_map/ppermute | solution.py:20
  163.3 9.2 %copy-start.3 = (f32[16,8,32,16]{2,3,1,0:T(8,128)S(1)}, f32[16,8,32,16]{2,3,1,0:T(8,128)}, u32[]{:S(2)}) copy-start(f32[16,8,32,16]{2,3,1,0:T(8,128)} %copy-done.2) | copy-start | bytes 786436
  163.3 9.2 %copy-start.11 = (bf16[8,16,16,64]{3,2,1,0:T(8,128)(2,1)S(1)}, bf16[8,16,16,64]{3,2,1,0:T(8,128)(2,1)}, u32[]{:S(2)}) copy-start(bf16[8,16,16,64]{3,2,1,0:T(8,128)(2,1)} %reshape.330) | copy-start | bytes 786436
  165.5 26.0 %collective-permute-start.4 = (f32[2,6,28,1024]{3,0,2,1:T(2,128)}, f32[2,6,28,1024]{3,0,2,1:T(2,128)}, u32[]{:S(2)}, u32[]{:S(2)}) collective-permute-start(f32[2,6,28,1024]{3,0,2,1:T(2,128)} %copy.138), channel_id=1, source_target_pairs={{0,32},{32,64},{64,96},{96,128},{128,160},{160,192},{192,224},{1,3... | collective-permute-start | bytes 4128776 | tf_op jit(solution)/shard_map/ppermute | solution.py:18
  193.4 11.1 %copy-start.12 = (f32[8,16,1024]{2,1,0:T(8,128)S(1)}, f32[8,16,1024]{2,1,0:T(8,128)}, u32[]{:S(2)}) copy-start(f32[8,16,1024]{2,1,0:T(8,128)} %scatter.4) | copy-start | bytes 1572868
  195.8 219.1 %collective-permute-start.7 = (bf16[2,8,6,1024]{3,2,1,0:T(8,128)(2,1)S(1)}, bf16[2,8,6,1024]{3,2,1,0:T(8,128)(2,1)S(1)}, u32[]{:S(2)}, u32[]{:S(2)}) collective-permute-start(bf16[2,8,6,1024]{3,2,1,0:T(8,128)(2,1)S(1)} %get-tuple-element.99), channel_id=1, source_target_pairs={{1,0},{2,1},{3,2},{4,3},{5,4},{6,5},{7,6},{8,7},{9,8},{10,9},{11,1... | collective-permute-start | bytes 589832 | tf_op jit(solution)/shard_map/ppermute | solution.py:20
  204.5 210.3 %collective-permute-start.6 = (bf16[2,8,6,1024]{3,2,1,0:T(8,128)(2,1)S(1)}, bf16[2,8,6,1024]{3,2,1,0:T(8,128)(2,1)}, u32[]{:S(2)}, u32[]{:S(2)}) collective-permute-start(bf16[2,8,6,1024]{3,2,1,0:T(8,128)(2,1)S(1)} %get-tuple-element.98), channel_id=1, source_target_pairs={{0,1},{1,2},{2,3},{3,4},{4,5},{5,6},{6,7},{7,8},{8,9},{9,10},{10,1... | collective-permute-start | bytes 589832 | tf_op jit(solution)/shard_map/ppermute | solution.py:18
  206.7 209.7 %copy-start.29 = (pred[16]{0:T(512)(128)(4,1)S(1)}, pred[16]{0:T(512)(128)(4,1)}, u32[]{:S(2)}) copy-start(pred[16]{0:T(512)(128)(4,1)} %constant.174.clone.1) | copy-start | bytes 52
  (20 other events, 75.6 us)
Sparse Core Ops, SparseCore 0:
  10.5 77.8 all-gather.2
  182.3 231.1 all-reduce.5
where the time goes:
time: 430 us; the launch traced here: 425 us
  waiting for transfers between devices  215 us (50%)
  local copies, waits for them, and re-layouts  93.6 us (22%)
  matrix products  54.5 us (13%)
  starting transfers between devices  25.1 us (6%)
  other arithmetic  21.2 us (5%)
  between operations  14.9 us (3%)
    unnamed x3, waiting for transfers between devices  206 us
    dot_general x1, matrix products, window_mask(): jnp.einsum('hrkb,cjb->hrckj', partial_rows, jnp.asarray(col_select), prec...  24.2 us
    gt x2, local copies, waits for them, and re-layouts, window_mask(): return full.reshape(head_count, count_q, count_k) > 0.5  14.8 us
    ppermute x4, starting transfers between devices, with_halo(): lax.ppermute(head, axis, [((i + 1) % count, i) for i in range(ends)])  14.6 us
    ppermute x4, starting transfers between devices, with_halo(): lax.ppermute(tail, axis, [(i, (i + 1) % count) for i in range(ends)])  10.4 us
    another operation x2, local copies, waits for them, and re-layouts, body(): jnp.stack([key_grad, value_grad])  8.74 us
  transfers between devices with their start and end apart: 10, of which 5 were waited for; matrix products, arithmetic and copies ran while one was open for 24% of the time, Pallas kernels for 0%

commit v1 on v0

v1 whole, which is shorter than its diff:
```python
import jax
import jax.numpy as jnp
from jax import lax
from jax.experimental import pallas as pl
from jax.experimental.pallas import tpu as pltpu
from jax.sharding import PartitionSpec as P

MESH = pl.DeviceIdType.MESH
RADIUS = 6
SPAN = 2 * RADIUS + 1
ROWS = 8
COLS = 16
REGION = ROWS + 2 * RADIUS
SECT = 32
ZN = 8
LANES = 256
CHUNKS = 4
TILES = 56
CENTRE, LEFT, RIGHT, ZONAL = 0, 20, 30, 40
NEVER = -1e30
BF, F32 = jnp.bfloat16, jnp.float32


def kernel(
    q_ref, k_ref, v_ref, do_ref, near_ref, zonal_ref,
    att_ref, gq_ref, gk_ref, gv_ref,
    kv, edge, corner, gath, bias, bias_z, wide, scores, probs,
    acc, side_out, side_in, lat_out, lat_in,
    z_out, z_in1, z_mid1, z_in2, z_mid2, z_in3,
    lat_s, lat_r, edge_s, edge_r, cor_s, cor_r,
    g_s, g_r, gy_s, gy_r, gc_s, gc_r, gd_s, gd_r,
    side_s, side_r, glat_s, glat_r, zc_s, zc_r, zy_s, zy_r, zz_s, zz_r,
):
    lat, lon = lax.axis_index("lat"), lax.axis_index("lon")
    lats, lons = lax.axis_size("lat"), lax.axis_size("lon")
    core, zed, why = lon % 2, (lon // 2) % ZN, lon // (2 * ZN)

    def lon_of(y, z, c):
        return (y * ZN + z) * 2 + c

    up, down = (lat + lats - 1) % lats, (lat + 1) % lats
    west, east = (lon + lons - 1) % lons, (lon + 1) % lons
    core_peer = lon_of(why, zed, 1 - core)
    y_peer = lon_of(1 - why, zed, core)
    z_peers = [None] + [lon_of(why, (zed + d) % ZN, core) for d in range(1, ZN)]
    z_from = [lon_of(why, (zed + ZN - d) % ZN, core) for d in range(ZN)]

    barrier = pltpu.get_barrier_semaphore()
    greeted = [(up, lon), (down, lon), (lat, west), (lat, east), (lat, core_peer), (lat, y_peer)]
    greeted += [(lat, peer) for peer in z_peers[1:]]
    for peer in greeted:
        pl.semaphore_signal(barrier, inc=1, device_id=peer, device_id_type=MESH)

    def remote(src, dst, send, recv, peer):
        return pltpu.make_async_remote_copy(
            src_ref=src, dst_ref=dst, send_sem=send, recv_sem=recv, device_id=peer, device_id_type=MESH
        )

    def lanes(c):
        return pl.ds(pl.multiple_of(c * LANES, LANES), LANES)

    def lat_copies(c):
        below = [
            remote(ref.at[2:8, :, lanes(c)], kv.at[c, i, 0:6], lat_s.at[c, i], lat_r.at[c, i], (down, lon))
            for i, ref in enumerate((k_ref, v_ref))
        ]
        above = [
            remote(ref.at[0:6, :, lanes(c)], kv.at[c, i, 14:20], lat_s.at[c, 2 + i], lat_r.at[c, 2 + i], (up, lon))
            for i, ref in enumerate((k_ref, v_ref))
        ]
        return below, above

    def edge_copies(c):
        return [
            remote(edge.at[c, 0], kv.at[c, :, LEFT + 3 : LEFT + 7], edge_s.at[c, 0], edge_r.at[c, 0], (lat, east)),
            remote(edge.at[c, 1], kv.at[c, :, RIGHT + 3 : RIGHT + 7], edge_s.at[c, 1], edge_r.at[c, 1], (lat, west)),
        ]

    def corner_copies(c):
        out = []
        for i, (base, peer) in enumerate(((LEFT, east), (RIGHT, west))):
            for j, first in enumerate((0, 7)):
                n = 2 * i + j
                out.append(
                    remote(
                        corner.at[c, i, j], kv.at[c, :, base + first : base + first + 3],
                        cor_s.at[c, n], cor_r.at[c, n], (lat, peer),
                    )
                )
        return out

    def gather_z(d):
        return remote(gath.at[lon], gath.at[lon], g_s.at[d], g_r.at[d], (lat, z_peers[d]))

    def gather_z_wait(d):
        return remote(gath.at[z_from[d]], gath.at[z_from[d]], g_s.at[d], g_r.at[d], (lat, z_peers[d]))

    def gather_y(d):
        return remote(gath.at[z_from[d]], gath.at[z_from[d]], gy_s.at[d], gy_r.at[d], (lat, y_peer))

    def gather_c(d):
        return remote(gath.at[z_from[d]], gath.at[z_from[d]], gc_s.at[d], gc_r.at[d], (lat, core_peer))

    def other_y(d):
        return lon_of(1 - why, (zed + ZN - d) % ZN, core)

    def gather_d(d):
        at = gath.at[other_y(d)]
        return remote(at, at, gd_s.at[d], gd_r.at[d], (lat, core_peer))

    def gather_y_wait(d):
        at = gath.at[other_y(d)]
        return remote(at, at, gy_s.at[d], gy_r.at[d], (lat, y_peer))

    def gather_c_wait(d):
        at = gath.at[lon_of(why, (zed + ZN - d) % ZN, 1 - core)]
        return remote(at, at, gc_s.at[d], gc_r.at[d], (lat, core_peer))

    def gather_d_wait(d):
        at = gath.at[lon_of(1 - why, (zed + ZN - d) % ZN, 1 - core)]
        return remote(at, at, gd_s.at[d], gd_r.at[d], (lat, core_peer))

    def side_copies(c):
        return [
            remote(side_out.at[c, 0], side_in.at[c, 0], side_s.at[c, 0], side_r.at[c, 0], (lat, west)),
            remote(side_out.at[c, 1], side_in.at[c, 1], side_s.at[c, 1], side_r.at[c, 1], (lat, east)),
        ]

    def grad_lat_copies(c):
        return [
            remote(lat_out.at[c, 0], lat_in.at[c, 0], glat_s.at[c, 0], glat_r.at[c, 0], (up, lon)),
            remote(lat_out.at[c, 1], lat_in.at[c, 1], glat_s.at[c, 1], glat_r.at[c, 1], (down, lon)),
        ]

    def zonal_core(c):
        return remote(z_out.at[c, 1 - core], z_in1.at[c], zc_s.at[c], zc_r.at[c], (lat, core_peer))

    def zonal_y(c):
        src = z_mid1.at[c, pl.ds((1 - why) * ZN, ZN)]
        return remote(src, z_in2.at[c], zy_s.at[c], zy_r.at[c], (lat, y_peer))

    def zonal_z(c, d):
        src = z_mid2.at[c, (zed + d) % ZN]
        return remote(src, z_in3.at[c, d], zz_s.at[c, d], zz_r.at[c, d], (lat, z_peers[d]))

    for i, ref in enumerate((k_ref, v_ref)):
        total = jnp.sum(ref[...].astype(F32), axis=1) * (COLS ** -0.5)
        if i == 0:
            pooled_keys = total
    gath[lon] = jnp.concatenate([pooled_keys, total], axis=0).astype(BF)

    def pack_edges(c):
        for i, ref in enumerate((k_ref, v_ref)):
            block = ref[:, :, lanes(c)].astype(F32)
            edge[c, 0, i] = block[:, 8:16].reshape(64, LANES).astype(BF).reshape(4, 16, LANES)
            edge[c, 1, i] = block[:, 0:8].reshape(64, LANES).astype(BF).reshape(4, 16, LANES)

    @pl.loop(0, CHUNKS)
    def _(c):
        pack_edges(c)

    pl.semaphore_wait(barrier, len(greeted))

    @pl.loop(0, CHUNKS)
    def _(c):
        below, above = lat_copies(c)

        @pl.when(lat < lats - 1)
        def _():
            for copy in below:
                copy.start()

        @pl.when(lat > 0)
        def _():
            for copy in above:
                copy.start()

    for d in (4, 3, 5, 2, 6, 1, 7):
        gather_z(d).start()
    gather_y(0).start()
    gather_c(0).start()

    @pl.loop(0, CHUNKS)
    def _(c):
        for copy in edge_copies(c):
            copy.start()

    @pl.loop(0, CHUNKS)
    def _(c):
        for i, ref in enumerate((k_ref, v_ref)):
            kv[c, i, 6:14] = ref[:, :, lanes(c)]

        @pl.when(lat == 0)
        def _():
            kv[c, :, 0:6] = jnp.zeros((2, 6, 16, LANES), BF)
            lat_in[c, 1] = jnp.zeros((2, 6, 16, LANES), BF)

        @pl.when(lat == lats - 1)
        def _():
            kv[c, :, 14:20] = jnp.zeros((2, 6, 16, LANES), BF)
            lat_in[c, 0] = jnp.zeros((2, 6, 16, LANES), BF)

    span_a = lax.broadcasted_iota(jnp.int32, (SPAN, 512), 0)
    lane_j = lax.broadcasted_iota(jnp.int32, (SPAN, 512), 1) // COLS
    select_a = ((REGION - 1 - lane_j) == span_a).astype(F32)
    centre = (lax.broadcasted_iota(jnp.int32, (SPAN, SPAN), 0) == RADIUS) & (
        lax.broadcasted_iota(jnp.int32, (SPAN, SPAN), 1) == RADIUS
    )
    sub = lax.broadcasted_iota(jnp.int32, (32, 512), 0)
    place = jnp.where(sub < 16, sub, jnp.where(sub < 24, sub - 24, sub - 8))
    offset = place - lax.broadcasted_iota(jnp.int32, (32, 512), 1) % COLS + RADIUS
    top_open = jnp.where(lat > 0, 0.0, NEVER).astype(F32)
    low_open = jnp.where(lat < lats - 1, 0.0, NEVER).astype(F32)

    def build_mask(pair):
        for half in range(2):
            head = near_ref[pair * 2 + half]
            allowed = jnp.where((head == 1) | centre, 1.0, 0.0).astype(F32)
            by_lane = lax.dot_general(
                allowed, select_a, (((0,), (0,)), ((), ())), preferred_element_type=F32
            )
            full = jnp.full((32, 512), NEVER, F32)
            by_lane = (by_lane - 1.0) * (-NEVER)
            for b in range(SPAN):
                full = jnp.where(offset == b, by_lane[b : b + 1, :], full)
            wide[...] = full
            for row in range(REGION):
                start = (REGION - 1 - row) * COLS
                tile, phase = start // 128, start % 128
                if phase:
                    both = wide[:, tile * 128 : tile * 128 + 256]
                    part = pltpu.roll(both, 256 - phase, 1)[:, 0:128]
                else:
                    part = wide[:, tile * 128 : tile * 128 + 128]
                if row < RADIUS:
                    part = jnp.minimum(part, top_open)
                if row >= ROWS + RADIUS:
                    part = jnp.minimum(part, low_open)
                at = slice(half * 128, half * 128 + 128)
                bias[pair, row * 16 : row * 16 + 16, at] = part[0:16]
                bias[pair, 320 + row * 8 : 328 + row * 8, at] = part[16:24]
                bias[pair, 480 + row * 8 : 488 + row * 8, at] = part[24:32]

    @pl.loop(0, 4)
    def _(pair):
        build_mask(pair)

    for d in (1, 7, 2, 6, 3, 5, 4):
        gather_z_wait(d).wait_recv()
        gather_y(d).start()
        gather_c(d).start()

    @pl.loop(4, 8)
    def _(pair):
        build_mask(pair)

    row_of_lane = lax.broadcasted_iota(jnp.int32, (ROWS, 128), 1) // COLS
    row_hot = (row_of_lane == lax.broadcasted_iota(jnp.int32, (ROWS, 128), 0)).astype(F32)
    zonal_ok = jnp.where(zonal_ref[...] == 1, 1.0, 0.0).astype(F32)
    by_sector = lax.dot_general(zonal_ok, row_hot, (((0,), (0,)), ((), ())), preferred_element_type=F32)
    for s in range(SECT):
        bias_z[s * 8 : s * 8 + 8, :] = (by_sector[s : s + 1, :] * row_hot - 1.0) * (-NEVER)

    @pl.loop(0, CHUNKS)
    def _(c):
        below, above = lat_copies(c)

        @pl.when(lat > 0)
        def _():
            for copy in below:
                copy.wait_recv()

        @pl.when(lat < lats - 1)
        def _():
            for copy in above:
                copy.wait_recv()

        for i in range(2):
            for j, first in enumerate((0, 14)):
                block = kv[c, i, first : first + 6].astype(F32)
                corner[c, 0, j, i] = block[:, 8:16].reshape(48, LANES).astype(BF).reshape(3, 16, LANES)
                corner[c, 1, j, i] = block[:, 0:8].reshape(48, LANES).astype(BF).reshape(3, 16, LANES)
        for copy in corner_copies(c):
            copy.start()

    for d in (0, 1, 7, 2, 6, 3, 5, 4):
        gather_y_wait(d).wait_recv()
        gather_d(d).start()
    for d in range(ZN):
        gather_c_wait(d).wait_recv()
    for d in range(ZN):
        gather_d_wait(d).wait_recv()

    low_half = lax.broadcasted_iota(jnp.int32, (128, 128), 1) < 64

    def split_pair(block):
        zero = jnp.zeros_like(block)
        both = jnp.concatenate([jnp.where(low_half, block, zero), jnp.where(low_half, zero, block)], axis=0)
        return both.astype(BF)

    def own_heads(product):
        return jnp.concatenate([product[0:64, 0:128], product[64:128, 128:256]], axis=0)

    NT = (((1,), (1,)), ((), ()))
    NN = (((1,), (0,)), ((), ()))
    TN = (((0,), (0,)), ((), ()))
    STEPS = TILES // 8

    def attend(c, half):
        here = pl.ds(pl.multiple_of(half * 128, 128), 128)
        there = pl.ds(pl.multiple_of(c * LANES + half * 128, 128), 128)
        pair = c * 2 + half
        q_both = split_pair(q_ref[:, :, there].reshape(128, 128).astype(F32) * 0.125)
        grad = do_ref[:, :, there].reshape(128, 128).astype(F32)
        grad_both = split_pair(grad)

        def tokens(i, t):
            return kv[c, i, t * 8 : t * 8 + 8, :, here].reshape(128, 128)

        highest = jnp.full((8, 256), NEVER, F32)
        for t in range(STEPS):
            s = lax.dot_general(tokens(0, t), q_both, NT, preferred_element_type=F32)
            if t < 5:
                s = s + bias[pair, t * 128 : t * 128 + 128, :]
            else:
                z = bias_z[(t - 5) * 128 : (t - 4) * 128, :]
                s = s + jnp.concatenate([z, z], axis=1)
            scores[t * 128 : t * 128 + 128, :] = s
            highest = jnp.maximum(highest, jnp.max(s.reshape(16, 8, 256), axis=0))
        top = jnp.max(highest, axis=0, keepdims=True)
        total = jnp.zeros((8, 256), F32)
        for t in range(STEPS):
            e = jnp.exp(scores[t * 128 : t * 128 + 128, :] - top)
            scores[t * 128 : t * 128 + 128, :] = e
            total = total + jnp.sum(e.reshape(16, 8, 256), axis=0)
        inverse = 1.0 / jnp.sum(total, axis=0, keepdims=True)
        out = jnp.zeros((128, 256), F32)
        for t in range(STEPS):
            p = scores[t * 128 : t * 128 + 128, :] * inverse
            scores[t * 128 : t * 128 + 128, :] = p
            p = p.astype(BF)
            probs[t * 128 : t * 128 + 128, :] = p
            out = out + lax.dot_general(tokens(1, t), p, TN, preferred_element_type=F32)
        out = own_heads(out)
        att_ref[:, :, there] = out.T.astype(BF).reshape(8, 16, 128)
        prod = out * grad.T
        delta = jnp.concatenate(
            [jnp.sum(prod[0:64], axis=0, keepdims=True), jnp.sum(prod[64:128], axis=0, keepdims=True)], axis=1
        )
        grad_q = jnp.zeros((128, 256), F32)
        for t in range(STEPS):
            dp = lax.dot_general(tokens(1, t), grad_both, NT, preferred_element_type=F32)
            ds = (scores[t * 128 : t * 128 + 128, :] * (dp - delta)).astype(BF)
            grad_q = grad_q + lax.dot_general(tokens(0, t), ds, TN, preferred_element_type=F32)
            dk = lax.dot_general(ds, q_both, NN, preferred_element_type=F32)
            dv = lax.dot_general(probs[t * 128 : t * 128 + 128, :], grad_both, NN, preferred_element_type=F32)
            if t < 5:
                for i, d in enumerate((dk, dv)):
                    d = d.reshape(8, 16, 128)
                    for n, (lo, hi) in enumerate(((CENTRE, LEFT), (LEFT, RIGHT), (RIGHT, ZONAL))):
                        first, last = max(lo, t * 8), min(hi, t * 8 + 8)
                        if first >= last:
                            continue
                        piece = d[first - t * 8 : last - t * 8]
                        if n == 0:
                            acc[c, i, first:last, :, here] = piece
                        else:
                            side_out[c, n - 1, i, first - lo : last - lo, :, here] = piece.astype(BF)
            else:
                both = jnp.concatenate([dk.reshape(16, 8, 128), dv.reshape(16, 8, 128)], axis=1)
                both = both.astype(BF).reshape(8, 2, 16, 128)
                for n in range(2):
                    z_out[c, n, (t - 5) * 8 : (t - 4) * 8, :, here] = both[:, n]
        grad_q = own_heads(grad_q) * 0.125
        gq_ref[:, :, there] = grad_q.T.astype(BF).reshape(8, 16, 128)

    def stage1(c):
        block = gath[:, :, lanes(c)].astype(F32)
        for i in range(2):
            rows = block[:, i * 8 : i * 8 + 8].reshape(SECT * 8, LANES).astype(BF)
            kv[c, i, ZONAL:TILES] = rows.reshape(16, 16, LANES)
        for copy in edge_copies(c) + corner_copies(c):
            copy.wait_recv()

        @pl.loop(0, 2)
        def _(half):
            attend(c, half)

        for copy in side_copies(c):
            copy.start()
        zonal_core(c).start()

    def stage2(c):
        for copy in side_copies(c):
            copy.wait_recv()
        for i in range(2):
            from_east = side_in[c, 0, i].astype(F32).reshape(REGION, 8, LANES)
            from_west = side_in[c, 1, i].astype(F32).reshape(REGION, 8, LANES)
            total = acc[c, i] + jnp.concatenate([from_west, from_east], axis=1)
            acc[c, i, 6:14] = total[6:14]
            lat_out[c, 0, i] = total[0:6].astype(BF)
            lat_out[c, 1, i] = total[14:20].astype(BF)
        to_up, to_down = grad_lat_copies(c)

        @pl.when(lat > 0)
        def _():
            to_up.start()

        @pl.when(lat < lats - 1)
        def _():
            to_down.start()

        zonal_core(c).wait_recv()
        z_mid1[c] = (z_out[c, core].astype(F32) + z_in1[c].astype(F32)).astype(BF)
        zonal_y(c).start()

    def stage3(c):
        zonal_y(c).wait_recv()
        z_mid2[c] = (z_mid1[c, pl.ds(why * ZN, ZN)].astype(F32) + z_in2[c].astype(F32)).astype(BF)
        for d in (4, 3, 5, 2, 6, 1, 7):
            zonal_z(c, d).start()

    def stage4(c):
        total = z_mid2[c, zed].astype(F32)
        for d in (1, 7, 2, 6, 3, 5, 4):
            zonal_z(c, d).wait_recv()
            total = total + z_in3[c, d].astype(F32)
        total = total * (COLS ** -0.5)
        to_up, to_down = grad_lat_copies(c)

        @pl.when(lat < lats - 1)
        def _():
            to_up.wait_recv()

        @pl.when(lat > 0)
        def _():
            to_down.wait_recv()

        for i, ref in enumerate((gk_ref, gv_ref)):
            for r in range(ROWS):
                row = acc[c, i, 6 + r] + total[i * 8 + r : i * 8 + r + 1, :]
                if r >= 2:
                    row = row + lat_in[c, 0, i, r - 2].astype(F32)
                if r < 6:
                    row = row + lat_in[c, 1, i, r].astype(F32)
                ref[r, :, lanes(c)] = row.astype(BF)

    @pl.loop(0, CHUNKS + 3)
    def _(step):
        @pl.when(step < CHUNKS)
        def _():
            stage1(step)

        @pl.when((step >= 1) & (step < CHUNKS + 1))
        def _():
            stage2(step - 1)

        @pl.when((step >= 2) & (step < CHUNKS + 2))
        def _():
            stage3(step - 2)

        @pl.when(step >= 3)
        def _():
            stage4(step - 3)

    @pl.loop(0, CHUNKS)
    def _(c):
        below, above = lat_copies(c)
        to_up, to_down = grad_lat_copies(c)

        @pl.when(lat < lats - 1)
        def _():
            for copy in below + [to_down]:
                copy.wait_send()

        @pl.when(lat > 0)
        def _():
            for copy in above + [to_up]:
                copy.wait_send()

        for copy in edge_copies(c) + corner_copies(c) + side_copies(c) + [zonal_core(c), zonal_y(c)]:
            copy.wait_send()
        for d in range(1, ZN):
            zonal_z(c, d).wait_send()

    for d in range(ZN):
        if d > 0:
            gather_z(d).wait_send()
        gather_y(d).wait_send()
        gather_c(d).wait_send()
        gather_d(d).wait_send()


def body(queries, keys, values, cotangent, near_pattern, zonal_pattern):
    block = jax.ShapeDtypeStruct(queries.shape, BF)
    dma = pltpu.SemaphoreType.DMA
    vm = pltpu.VMEM
    scratch = [
        vm((CHUNKS, 2, TILES, 16, LANES), BF),
        vm((CHUNKS, 2, 2, 4, 16, LANES), BF),
        vm((CHUNKS, 2, 2, 2, 3, 16, LANES), BF),
        vm((SECT, 16, 1024), BF),
        vm((8, 640, 256), F32),
        vm((SECT * 8, 128), F32),
        vm((32, 512), F32),
        vm((TILES * 16, 256), F32),
        vm((TILES * 16, 256), BF),
        vm((CHUNKS, 2, REGION, 16, LANES), F32),
        vm((CHUNKS, 2, 2, 10, 16, LANES), BF),
        vm((CHUNKS, 2, 2, 10, 16, LANES), BF),
        vm((CHUNKS, 2, 2, 6, 16, LANES), BF),
        vm((CHUNKS, 2, 2, 6, 16, LANES), BF),
        vm((CHUNKS, 2, 16, 16, LANES), BF),
        vm((CHUNKS, 16, 16, LANES), BF),
        vm((CHUNKS, 16, 16, LANES), BF),
        vm((CHUNKS, 8, 16, LANES), BF),
        vm((CHUNKS, 8, 16, LANES), BF),
        vm((CHUNKS, 8, 16, LANES), BF),
    ]
    sems = [(CHUNKS, 4), (CHUNKS, 2), (CHUNKS, 4), (ZN,), (ZN,), (ZN,), (ZN,), (CHUNKS, 2), (CHUNKS, 2), (CHUNKS,), (CHUNKS,), (CHUNKS, ZN)]
    for shape in sems:
        scratch += [dma(shape), dma(shape)]
    return pl.pallas_call(
        kernel,
        out_shape=[block] * 4,
        in_specs=[pl.BlockSpec(memory_space=pltpu.VMEM)] * 6,
        out_specs=[pl.BlockSpec(memory_space=pltpu.VMEM)] * 4,
        scratch_shapes=scratch,
        compiler_params=pltpu.CompilerParams(
            collective_id=0, has_side_effects=True, vmem_limit_bytes=56 * 1024 * 1024
        ),
        cost_estimate=pl.CostEstimate(flops=3_000_000_000, bytes_accessed=2 << 20, transcendentals=1 << 20),
    )(queries, keys, values, cotangent, near_pattern, zonal_pattern)


def solution(mesh):
    grid = P("lat", "lon", None)
    return jax.shard_map(
        body,
        mesh=mesh,
        in_specs=(grid, grid, grid, grid, P(), P("lat", None)),
        out_specs=(grid, grid, grid, grid),
        check_vma=False,
    )
```

time: 430 us -> 79.2 us (0.18); the launches traced: 425 us -> 79 us
  waiting for transfers between devices: 215 us -> 0 us
  local copies, waits for them, and re-layouts: 93.6 us -> 6.1 us
  Pallas kernels: 0 us -> 72.2 us
  matrix products: 54.5 us -> 0 us
  starting transfers between devices: 25.1 us -> 0 us
  other arithmetic: 21.2 us -> 0 us
  between operations: 14.9 us -> 0.65 us
    unnamed x3 -> x0, waiting for transfers between devices: 206 us -> none
    pallas_call x0 -> x1, Pallas kernels: none -> 72.2 us  [body(): pl.pallas_call(kernel, out_shape=[block] * 4, in_specs=[pl.BlockSpec(memo...]
    dot_general x14 -> x0, matrix products: 54.5 us -> none  [the longest x1 24.2 us: window_mask(): jnp.einsum('hrkb,cjb->hrckj', partial_rows, jnp.asarray(col_select), prec...]
    ppermute x8 -> x0, starting transfers between devices: 25 us -> none  [the longest x4 14.6 us: with_halo(): lax.ppermute(head, axis, [((i + 1) % count, i) for i in range(ends)])]
    another operation x7 -> x0, local copies, waits for them, and re-layouts: 15.1 us -> none  [the longest x2 8.74 us: body(): jnp.stack([key_grad, value_grad])]
    gt x2 -> x0, local copies, waits for them, and re-layouts: 14.8 us -> none  [window_mask(): return full.reshape(head_count, count_q, count_k) > 0.5]
    squeeze x4 -> x0, local copies, waits for them, and re-layouts: 14 us -> none  [the longest x2 7.1 us: body(): kv_block[1]]
    transpose x7 -> x0, local copies, waits for them, and re-layouts: 13.3 us -> none  [the longest x1 5.74 us: body(): jnp.einsum('hqk,qhd->khd', grad_scores, query_tile, preferred_element_typ...]
  transfers between devices with their start and end apart: 10 -> 0, of which waited for: 5 -> 0; matrix products, arithmetic and copies ran while one was open for 24% -> 0% of each run, Pallas kernels for 0% -> 0%
where the time goes in v1:
time: 79.2 us; the launch traced here: 79 us
  Pallas kernels  72.2 us (91%)
  local copies, waits for them, and re-layouts  6.1 us (8%)
    pallas_call x1, Pallas kernels, body(): pl.pallas_call(kernel, out_shape=[block] * 4, in_specs=[pl.BlockSpec(memo...  72.2 us
    unnamed x11, local copies, waits for them, and re-layouts  6.1 us

profile of v1, /device:TPU:1, one launch (start us, length us, event | category | flops | bytes accessed | tf_op | source)
XLA Modules:
  0.0 79.0 jit_solution(3780438738757465439)
XLA Ops:
  0.6 1.6 %copy.10.near_ref = s32[16,13,13]{2,1,0:T(8,128)} copy(s32[16,13,13]{2,0,1:T(8,128)} %param.10) | data formatting | bytes 21632 | tf_op args[4]
  2.2 72.2 %shard_map.93 = (bf16[8,16,1024]{2,1,0:T(8,128)(2,1)}, bf16[8,16,1024]{2,1,0:T(8,128)(2,1)}, bf16[8,16,1024]{2,1,0:T(8,128)(2,1)}, bf16[8,16,1024]{2,1,0:T(8,128)(2,1)}) custom-call(bf16[8,16,1024]{2,1,0:T(8,128)(2,1)} %q_ref.1, bf16[8,16,1024]{2,1,0:T(8,128)(2,1)} %k_ref.1, bf16[8,16,1024]{2,1,0:T(8,128)(2,1)} %v_ref.1, bf16[8,16,1024]{2,1,0:T(8,128)(2,1)} %do_ref.1, ...), custom_call_target="tpu_custom_call" | custom-call | flops 3000000000 | bytes 2097152 | tf_op jit(solution)/shard_map/pallas_call | solution.py:523
  74.4 0.0 copy-start.2
  74.5 1.7 %copy.15 = bf16[8,16,1024]{2,1,0:T(8,128)(2,1)} copy(bf16[8,16,1024]{2,1,0:T(8,128)(2,1)} %get-tuple-element.8) | data formatting | bytes 524288
  76.2 0.0 copy-done.2
  76.2 0.0 copy-start.1
  76.2 0.7 copy.16
  76.9 0.3 copy-done.1
  77.2 0.0 copy-start
  77.2 0.7 copy.17
  77.9 0.3 copy-done
  78.3 0.7 copy.18
Async XLA Ops:
  74.4 1.7 %copy-start.2 = (bf16[8,16,1024]{2,1,0:T(8,128)(2,1)S(1)}, bf16[8,16,1024]{2,1,0:T(8,128)(2,1)}, u32[]{:S(2)}) copy-start(bf16[8,16,1024]{2,1,0:T(8,128)(2,1)} %get-tuple-element.9) | copy-start | bytes 786436
  76.2 1.0 %copy-start.1 = (bf16[8,16,1024]{2,1,0:T(8,128)(2,1)S(1)}, bf16[8,16,1024]{2,1,0:T(8,128)(2,1)}, u32[]{:S(2)}) copy-start(bf16[8,16,1024]{2,1,0:T(8,128)(2,1)} %get-tuple-element.10) | copy-start | bytes 786436
  77.2 1.0 %copy-start = (bf16[8,16,1024]{2,1,0:T(8,128)(2,1)S(1)}, bf16[8,16,1024]{2,1,0:T(8,128)(2,1)}, u32[]{:S(2)}) copy-start(bf16[8,16,1024]{2,1,0:T(8,128)(2,1)} %get-tuple-element.11) | copy-start | bytes 786436

commit v2 on v1

--- a/solution.py
+++ b/solution.py
@@ -27,8 +27,9 @@
     kv, edge, corner, gath, bias, bias_z, wide, scores, probs,
     acc, side_out, side_in, lat_out, lat_in,
     z_out, z_in1, z_mid1, z_in2, z_mid2, z_in3,
+    relay, relay_g, rel_s, rel_r, fwd_s, fwd_r, relg_s, relg_r, fwdg_s, fwdg_r,
     lat_s, lat_r, edge_s, edge_r, cor_s, cor_r,
-    g_s, g_r, gy_s, gy_r, gc_s, gc_r, gd_s, gd_r,
+    g_s, g_r, gy_s, gy_r, gc_s, gc_r,
     side_s, side_r, glat_s, glat_r, zc_s, zc_r, zy_s, zy_r, zz_s, zz_r,
 ):
     lat, lon = lax.axis_index("lat"), lax.axis_index("lon")
@@ -43,7 +44,6 @@
     core_peer = lon_of(why, zed, 1 - core)
     y_peer = lon_of(1 - why, zed, core)
     z_peers = [None] + [lon_of(why, (zed + d) % ZN, core) for d in range(1, ZN)]
-    z_from = [lon_of(why, (zed + ZN - d) % ZN, core) for d in range(ZN)]
 
     barrier = pltpu.get_barrier_semaphore()
     greeted = [(up, lon), (down, lon), (lat, west), (lat, east), (lat, core_peer), (lat, y_peer)]
@@ -51,6 +51,18 @@
     for peer in greeted:
         pl.semaphore_signal(barrier, inc=1, device_id=peer, device_id_type=MESH)
 
+    middle = lats // 2
+    crosses = (lat == middle - 1) | (lat == middle)
+    far_down, far_up = lat == middle - 1, lat == middle
+
+    @pl.when(far_down)
+    def _():
+        pl.semaphore_signal(barrier, inc=1, device_id=(down, y_peer), device_id_type=MESH)
+
+    @pl.when(far_up)
+    def _():
+        pl.semaphore_signal(barrier, inc=1, device_id=(up, y_peer), device_id_type=MESH)
+
     def remote(src, dst, send, recv, peer):
         return pltpu.make_async_remote_copy(
             src_ref=src, dst_ref=dst, send_sem=send, recv_sem=recv, device_id=peer, device_id_type=MESH
@@ -69,6 +81,31 @@
             for i, ref in enumerate((k_ref, v_ref))
         ]
         return below, above
+
+    def cross_copies(c):
+        below = [
+            remote(ref.at[2:8, :, lanes(c)], relay.at[c, i], lat_s.at[c, i], rel_r.at[c, i], (down, y_peer))
+            for i, ref in enumerate((k_ref, v_ref))
+        ]
+        above = [
+            remote(ref.at[0:6, :, lanes(c)], relay.at[c, i], lat_s.at[c, 2 + i], rel_r.at[c, i], (up, y_peer))
+            for i, ref in enumerate((k_ref, v_ref))
+        ]
+        return below, above
+
+    def pass_on(c):
+        at = kv.at[c, :, pl.ds((middle - lat) * (REGION - 6), 6)]
+        return remote(relay.at[c], at, fwd_s.at[c], fwd_r.at[c], (lat, y_peer))
+
+    def cross_grads(c):
+        return [
+            remote(lat_out.at[c, 0], relay_g.at[c], glat_s.at[c, 0], relg_r.at[c], (up, y_peer)),
+            remote(lat_out.at[c, 1], relay_g.at[c], glat_s.at[c, 1], relg_r.at[c], (down, y_peer)),
+        ]
+
+    def pass_on_grads(c):
+        at = lat_in.at[c, lat - middle + 1]
+        return remote(relay_g.at[c], at, fwdg_s.at[c], fwdg_r.at[c], (lat, y_peer))
 
     def edge_copies(c):
         return [
@@ -89,36 +126,21 @@
                 )
         return out
 
-    def gather_z(d):
-        return remote(gath.at[lon], gath.at[lon], g_s.at[d], g_r.at[d], (lat, z_peers[d]))
-
-    def gather_z_wait(d):
-        return remote(gath.at[z_from[d]], gath.at[z_from[d]], g_s.at[d], g_r.at[d], (lat, z_peers[d]))
-
-    def gather_y(d):
-        return remote(gath.at[z_from[d]], gath.at[z_from[d]], gy_s.at[d], gy_r.at[d], (lat, y_peer))
-
-    def gather_c(d):
-        return remote(gath.at[z_from[d]], gath.at[z_from[d]], gc_s.at[d], gc_r.at[d], (lat, core_peer))
-
-    def other_y(d):
-        return lon_of(1 - why, (zed + ZN - d) % ZN, core)
-
-    def gather_d(d):
-        at = gath.at[other_y(d)]
-        return remote(at, at, gd_s.at[d], gd_r.at[d], (lat, core_peer))
-
-    def gather_y_wait(d):
-        at = gath.at[other_y(d)]
-        return remote(at, at, gy_s.at[d], gy_r.at[d], (lat, y_peer))
-
-    def gather_c_wait(d):
-        at = gath.at[lon_of(why, (zed + ZN - d) % ZN, 1 - core)]
-        return remote(at, at, gc_s.at[d], gc_r.at[d], (lat, core_peer))
-
-    def gather_d_wait(d):
-        at = gath.at[lon_of(1 - why, (zed + ZN - d) % ZN, 1 - core)]
-        return remote(at, at, gd_s.at[d], gd_r.at[d], (lat, core_peer))
+    def gather_y(y):
+        at = gath.at[:, core, y, zed]
+        return remote(at, at, gy_s.at[0], gy_r.at[0], (lat, y_peer))
+
+    def gather_z(c, d):
+        at = gath.at[c, core, :, zed]
+        return remote(at, at, g_s.at[c, d], g_r.at[c, d], (lat, z_peers[d]))
+
+    def gather_z_wait(c, d):
+        at = gath.at[c, core, :, (zed + ZN - d) % ZN]
+        return remote(at, at, g_s.at[c, d], g_r.at[c, d], (lat, z_peers[d]))
+
+    def gather_c(c, which):
+        at = gath.at[c, which]
+        return remote(at, at, gc_s.at[c], gc_r.at[c], (lat, core_peer))
 
     def side_copies(c):
         return [
@@ -147,7 +169,9 @@
         total = jnp.sum(ref[...].astype(F32), axis=1) * (COLS ** -0.5)
         if i == 0:
             pooled_keys = total
-    gath[lon] = jnp.concatenate([pooled_keys, total], axis=0).astype(BF)
+    pooled = jnp.concatenate([pooled_keys, total], axis=0).astype(BF)
+    for c in range(CHUNKS):
+        gath[c, core, why, zed] = pooled[:, c * LANES : (c + 1) * LANES]
 
     def pack_edges(c):
         for i, ref in enumerate((k_ref, v_ref)):
@@ -159,31 +183,46 @@
     def _(c):
         pack_edges(c)
 
-    pl.semaphore_wait(barrier, len(greeted))
-
-    @pl.loop(0, CHUNKS)
-    def _(c):
+    pl.semaphore_wait(barrier, len(greeted) + jnp.where(crosses, 1, 0))
+
+    def send_rows(c):
         below, above = lat_copies(c)
-
-        @pl.when(lat < lats - 1)
+        far_below, far_above = cross_copies(c)
+        near = c == 0
+
+        @pl.when((lat < lats - 1) & ((lat != middle - 1) | near))
         def _():
             for copy in below:
                 copy.start()
 
-        @pl.when(lat > 0)
+        @pl.when(far_down & (not near))
+        def _():
+            for copy in far_below:
+                copy.start()
+
+        @pl.when((lat > 0) & ((lat != middle) | near))
         def _():
             for copy in above:
                 copy.start()
 
-    for d in (4, 3, 5, 2, 6, 1, 7):
-        gather_z(d).start()
-    gather_y(0).start()
-    gather_c(0).start()
-
-    @pl.loop(0, CHUNKS)
-    def _(c):
+        @pl.when(far_up & (not near))
+        def _():
+            for copy in far_above:
+                copy.start()
+
+    def send(c):
         for copy in edge_copies(c):
             copy.start()
+
+    def send_pooled(c):
+        for d in (4, 3, 5, 2, 6, 1, 7):
+            gather_z(c, d).start()
+
+    gather_y(why).start()
+    send_rows(0)
+    send(0)
+    for c in range(1, CHUNKS):
+        send_rows(c)
 
     @pl.loop(0, CHUNKS)
     def _(c):
@@ -241,39 +280,40 @@
                 bias[pair, 320 + row * 8 : 328 + row * 8, at] = part[16:24]
                 bias[pair, 480 + row * 8 : 488 + row * 8, at] = part[24:32]
 
-    @pl.loop(0, 4)
-    def _(pair):
-        build_mask(pair)
-
-    for d in (1, 7, 2, 6, 3, 5, 4):
-        gather_z_wait(d).wait_recv()
-        gather_y(d).start()
-        gather_c(d).start()
-
-    @pl.loop(4, 8)
-    def _(pair):
-        build_mask(pair)
-
     row_of_lane = lax.broadcasted_iota(jnp.int32, (ROWS, 128), 1) // COLS
     row_hot = (row_of_lane == lax.broadcasted_iota(jnp.int32, (ROWS, 128), 0)).astype(F32)
-    zonal_ok = jnp.where(zonal_ref[...] == 1, 1.0, 0.0).astype(F32)
-    by_sector = lax.dot_general(zonal_ok, row_hot, (((0,), (0,)), ((), ())), preferred_element_type=F32)
-    for s in range(SECT):
-        bias_z[s * 8 : s * 8 + 8, :] = (by_sector[s : s + 1, :] * row_hot - 1.0) * (-NEVER)
-
-    @pl.loop(0, CHUNKS)
-    def _(c):
+
+    def build_zonal_mask():
+        zonal_ok = jnp.where(zonal_ref[...] == 1, 1.0, 0.0).astype(F32)
+        by_sector = lax.dot_general(zonal_ok, row_hot, (((0,), (0,)), ((), ())), preferred_element_type=F32)
+        for n in range(SECT):
+            s = n % 16 * 2 + n // 16
+            bias_z[n * 8 : n * 8 + 8, :] = (by_sector[s : s + 1, :] * row_hot - 1.0) * (-NEVER)
+
+    def relay_rows(c):
+        @pl.when(crosses)
+        def _():
+            for copy in cross_copies(c)[0]:
+                copy.wait_recv()
+            pass_on(c).start()
+
+    def prepare_a(c):
         below, above = lat_copies(c)
-
-        @pl.when(lat > 0)
+        near = c == 0
+
+        @pl.when((lat > 0) & ((lat != middle) | near))
         def _():
             for copy in below:
                 copy.wait_recv()
 
-        @pl.when(lat < lats - 1)
+        @pl.when((lat < lats - 1) & ((lat != middle - 1) | near))
         def _():
             for copy in above:
                 copy.wait_recv()
+
+        @pl.when(crosses & jnp.logical_not(near))
+        def _():
+            pass_on(c).wait_recv()
 
         for i in range(2):
             for j, first in enumerate((0, 14)):
@@ -283,13 +323,30 @@
         for copy in corner_copies(c):
             copy.start()
 
-    for d in (0, 1, 7, 2, 6, 3, 5, 4):
-        gather_y_wait(d).wait_recv()
-        gather_d(d).start()
-    for d in range(ZN):
-        gather_c_wait(d).wait_recv()
-    for d in range(ZN):
-        gather_d_wait(d).wait_recv()
+    def prepare_b(c):
+        for d in range(1, ZN):
+            gather_z_wait(c, d).wait_recv()
+        gather_c(c, core).start()
+
+    def build_masks(first, last):
+        @pl.loop(first, last)
+        def _(pair):
+            build_mask(pair)
+
+    build_masks(0, 4)
+    gather_y(1 - why).wait_recv()
+    send_pooled(0)
+    send(1)
+    build_zonal_mask()
+    build_masks(4, 8)
+    prepare_a(0)
+    send_pooled(1)
+    send(2)
+    relay_rows(1)
+    prepare_b(0)
+    relay_rows(2)
+    send(3)
+    prepare_a(1)
 
     low_half = lax.broadcasted_iota(jnp.int32, (128, 128), 1) < 64
 
@@ -368,29 +425,31 @@
                             side_out[c, n - 1, i, first - lo : last - lo, :, here] = piece.astype(BF)
             else:
                 both = jnp.concatenate([dk.reshape(16, 8, 128), dv.reshape(16, 8, 128)], axis=1)
-                both = both.astype(BF).reshape(8, 2, 16, 128)
-                for n in range(2):
-                    z_out[c, n, (t - 5) * 8 : (t - 4) * 8, :, here] = both[:, n]
+                z_out[c, t - 5, :, :, here] = both.astype(BF)
         grad_q = own_heads(grad_q) * 0.125
         gq_ref[:, :, there] = grad_q.T.astype(BF).reshape(8, 16, 128)
 
-    def stage1(c):
-        block = gath[:, :, lanes(c)].astype(F32)
-        for i in range(2):
-            rows = block[:, i * 8 : i * 8 + 8].reshape(SECT * 8, LANES).astype(BF)
-            kv[c, i, ZONAL:TILES] = rows.reshape(16, 16, LANES)
+    def load(c):
+        gather_c(c, 1 - core).wait_recv()
+        for first in range(2):
+            block = gath[c, first].reshape(16, 16, LANES).astype(F32)
+            for i in range(2):
+                rows = block[:, i * 8 : i * 8 + 8].reshape(128, LANES).astype(BF)
+                kv[c, i, ZONAL + first * 8 : ZONAL + first * 8 + 8] = rows.reshape(8, 16, LANES)
         for copy in edge_copies(c) + corner_copies(c):
             copy.wait_recv()
 
-        @pl.loop(0, 2)
-        def _(half):
-            attend(c, half)
-
+    def stage1(c):
+        zonal_core(c).start()
         for copy in side_copies(c):
             copy.start()
-        zonal_core(c).start()
-
-    def stage2(c):
+
+    def stage2_zonal(c):
+        zonal_core(c).wait_recv()
+        z_mid1[c] = (z_out[c, core].astype(F32) + z_in1[c].astype(F32)).astype(BF)
+        zonal_y(c).start()
+
+    def stage2_side(c):
         for copy in side_copies(c):
             copy.wait_recv()
         for i in range(2):
@@ -401,18 +460,30 @@
             lat_out[c, 0, i] = total[0:6].astype(BF)
             lat_out[c, 1, i] = total[14:20].astype(BF)
         to_up, to_down = grad_lat_copies(c)
-
-        @pl.when(lat > 0)
+        far_to_up, far_to_down = cross_grads(c)
+        near = c == CHUNKS - 1
+
+        @pl.when((lat > 0) & ((lat != middle) | near))
         def _():
             to_up.start()
 
-        @pl.when(lat < lats - 1)
+        @pl.when(far_up & jnp.logical_not(near))
+        def _():
+            far_to_up.start()
+
+        @pl.when((lat < lats - 1) & ((lat != middle - 1) | near))
         def _():
             to_down.start()
 
-        zonal_core(c).wait_recv()
-        z_mid1[c] = (z_out[c, core].astype(F32) + z_in1[c].astype(F32)).astype(BF)
-        zonal_y(c).start()
+        @pl.when(far_down & jnp.logical_not(near))
+        def _():
+            far_to_down.start()
+
+    def relay_grads(c):
+        @pl.when(crosses)
+        def _():
+            cross_grads(c)[0].wait_recv()
+            pass_on_grads(c).start()
 
     def stage3(c):
         zonal_y(c).wait_recv()
@@ -427,14 +498,19 @@
             total = total + z_in3[c, d].astype(F32)
         total = total * (COLS ** -0.5)
         to_up, to_down = grad_lat_copies(c)
-
-        @pl.when(lat < lats - 1)
+        near = c == CHUNKS - 1
+
+        @pl.when((lat < lats - 1) & ((lat != middle - 1) | near))
         def _():
             to_up.wait_recv()
 
-        @pl.when(lat > 0)
+        @pl.when((lat > 0) & ((lat != middle) | near))
         def _():
             to_down.wait_recv()
+
+        @pl.when(crosses & jnp.logical_not(near))
+        def _():
+            pass_on_grads(c).wait_recv()
 
         for i, ref in enumerate((gk_ref, gv_ref)):
             for r in range(ROWS):
@@ -445,23 +521,56 @@
                     row = row + lat_in[c, 1, i, r].astype(F32)
                 ref[r, :, lanes(c)] = row.astype(BF)
 
-    @pl.loop(0, CHUNKS + 3)
-    def _(step):
-        @pl.when(step < CHUNKS)
-        def _():
-            stage1(step)
-
-        @pl.when((step >= 1) & (step < CHUNKS + 1))
-        def _():
-            stage2(step - 1)
-
-        @pl.when((step >= 2) & (step < CHUNKS + 2))
-        def _():
-            stage3(step - 2)
-
-        @pl.when(step >= 3)
-        def _():
-            stage4(step - 3)
+    @pl.loop(0, CHUNKS)
+    def _(c):
+        load(c)
+
+        @pl.when(c == 0)
+        def _():
+            relay_rows(3)
+
+        attend(c, 0)
+
+        @pl.when(c < CHUNKS - 1)
+        def _():
+            prepare_b(c + 1)
+
+        @pl.when(c > 0)
+        def _():
+            stage2_zonal(c - 1)
+
+        @pl.when(c > 1)
+        def _():
+            stage3(c - 2)
+
+        @pl.when(c < CHUNKS - 2)
+        def _():
+            send_pooled(c + 2)
+            prepare_a(c + 2)
+
+        attend(c, 1)
+        stage1(c)
+
+        @pl.when(c > 0)
+        def _():
+            stage2_side(c - 1)
+
+        @pl.when(c > 1)
+        def _():
+            relay_grads(c - 2)
+
+        @pl.when(c > 2)
+        def _():
+            stage4(c - 3)
+
+    stage2_zonal(CHUNKS - 1)
+    stage3(CHUNKS - 2)
+    stage2_side(CHUNKS - 1)
+    relay_grads(CHUNKS - 2)
+    stage3(CHUNKS - 1)
+    stage4(1)
+    stage4(2)
+    stage4(3)
 
     @pl.loop(0, CHUNKS)
     def _(c):
@@ -478,17 +587,21 @@
             for copy in above + [to_up]:
                 copy.wait_send()
 
-        for copy in edge_copies(c) + corner_copies(c) + side_copies(c) + [zonal_core(c), zonal_y(c)]:
+        for copy in edge_copies(c) + corner_copies(c) + side_copies(c) + [zonal_core(c), zonal_y(c), gather_c(c, core)]:
             copy.wait_send()
         for d in range(1, ZN):
             zonal_z(c, d).wait_send()
-
-    for d in range(ZN):
-        if d > 0:
-            gather_z(d).wait_send()
-        gather_y(d).wait_send()
-        gather_c(d).wait_send()
-        gather_d(d).wait_send()
+            gather_z(c, d).wait_send()
+
+        @pl.when(crosses & (c > 0))
+        def _():
+            pass_on(c).wait_send()
+
+        @pl.when(crosses & (c < CHUNKS - 1))
+        def _():
+            pass_on_grads(c).wait_send()
+
+    gather_y(why).wait_send()
 
 
 def body(queries, keys, values, cotangent, near_pattern, zonal_pattern):
@@ -499,7 +612,7 @@
         vm((CHUNKS, 2, TILES, 16, LANES), BF),
         vm((CHUNKS, 2, 2, 4, 16, LANES), BF),
         vm((CHUNKS, 2, 2, 2, 3, 16, LANES), BF),
-        vm((SECT, 16, 1024), BF),
+        vm((CHUNKS, 2, 2, ZN, 16, LANES), BF),
         vm((8, 640, 256), F32),
         vm((SECT * 8, 128), F32),
         vm((32, 512), F32),
@@ -516,8 +629,10 @@
         vm((CHUNKS, 8, 16, LANES), BF),
         vm((CHUNKS, 8, 16, LANES), BF),
         vm((CHUNKS, 8, 16, LANES), BF),
+        vm((CHUNKS, 2, 6, 16, LANES), BF),
+        vm((CHUNKS, 2, 6, 16, LANES), BF),
     ]
-    sems = [(CHUNKS, 4), (CHUNKS, 2), (CHUNKS, 4), (ZN,), (ZN,), (ZN,), (ZN,), (CHUNKS, 2), (CHUNKS, 2), (CHUNKS,), (CHUNKS,), (CHUNKS, ZN)]
+    sems = [(CHUNKS, 2), (CHUNKS,), (CHUNKS,), (CHUNKS,), (CHUNKS, 4), (CHUNKS, 2), (CHUNKS, 4), (CHUNKS, ZN), (1,), (CHUNKS,), (CHUNKS, 2), (CHUNKS, 2), (CHUNKS,), (CHUNKS,), (CHUNKS, ZN)]
     for shape in sems:
         scratch += [dma(shape), dma(shape)]
     return pl.pallas_call(

time: 79.2 us -> 68.6 us (0.87)
  the two profiles are of different devices: /device:TPU:1 before, /device:TPU:24 now
where the time goes in v2:
time: 68.6 us; the launch traced here: 68.3 us
  Pallas kernels  61.6 us (90%)
  local copies, waits for them, and re-layouts  6.1 us (9%)
    pallas_call x1, Pallas kernels, body(): pl.pallas_call(kernel, out_shape=[block] * 4, in_specs=[pl.BlockSpec(memo...  61.6 us
    unnamed x11, local copies, waits for them, and re-layouts  6.1 us

profile of v2, /device:TPU:24, one launch (start us, length us, event | category | flops | bytes accessed | tf_op | source)
XLA Modules:
  0.0 68.3 jit_solution(6258988201625362103)
XLA Ops:
  0.6 1.6 %copy.10.near_ref = s32[16,13,13]{2,1,0:T(8,128)} copy(s32[16,13,13]{2,0,1:T(8,128)} %param.10) | data formatting | bytes 21632 | tf_op args[4]
  2.2 61.6 %shard_map.93 = (bf16[8,16,1024]{2,1,0:T(8,128)(2,1)}, bf16[8,16,1024]{2,1,0:T(8,128)(2,1)}, bf16[8,16,1024]{2,1,0:T(8,128)(2,1)}, bf16[8,16,1024]{2,1,0:T(8,128)(2,1)}) custom-call(bf16[8,16,1024]{2,1,0:T(8,128)(2,1)} %q_ref.1, bf16[8,16,1024]{2,1,0:T(8,128)(2,1)} %k_ref.1, bf16[8,16,1024]{2,1,0:T(8,128)(2,1)} %v_ref.1, bf16[8,16,1024]{2,1,0:T(8,128)(2,1)} %do_ref.1, ...), custom_call_target="tpu_custom_call" | custom-call | flops 3000000000 | bytes 2097152 | tf_op jit(solution)/shard_map/pallas_call | solution.py:638
  63.8 0.0 copy-start.2
  63.8 1.7 %copy.15 = bf16[8,16,1024]{2,1,0:T(8,128)(2,1)} copy(bf16[8,16,1024]{2,1,0:T(8,128)(2,1)} %get-tuple-element.8) | data formatting | bytes 524288
  65.5 0.0 copy-done.2
  65.6 0.0 copy-start.1
  65.6 0.7 %copy.16 = bf16[8,16,1024]{2,1,0:T(8,128)(2,1)} copy(bf16[8,16,1024]{2,1,0:T(8,128)(2,1)S(1)} %copy-done.2) | data formatting | bytes 524288
  66.3 0.3 copy-done.1
  66.6 0.0 copy-start
  66.6 0.7 %copy.17 = bf16[8,16,1024]{2,1,0:T(8,128)(2,1)} copy(bf16[8,16,1024]{2,1,0:T(8,128)(2,1)S(1)} %copy-done.1) | data formatting | bytes 524288
  67.3 0.3 copy-done
  67.6 0.7 %copy.18 = bf16[8,16,1024]{2,1,0:T(8,128)(2,1)} copy(bf16[8,16,1024]{2,1,0:T(8,128)(2,1)S(1)} %copy-done) | data formatting | bytes 524288
Async XLA Ops:
  63.8 1.7 %copy-start.2 = (bf16[8,16,1024]{2,1,0:T(8,128)(2,1)S(1)}, bf16[8,16,1024]{2,1,0:T(8,128)(2,1)}, u32[]{:S(2)}) copy-start(bf16[8,16,1024]{2,1,0:T(8,128)(2,1)} %get-tuple-element.9) | copy-start | bytes 786436
  65.6 1.0 %copy-start.1 = (bf16[8,16,1024]{2,1,0:T(8,128)(2,1)S(1)}, bf16[8,16,1024]{2,1,0:T(8,128)(2,1)}, u32[]{:S(2)}) copy-start(bf16[8,16,1024]{2,1,0:T(8,128)(2,1)} %get-tuple-element.10) | copy-start | bytes 786436
  66.6 1.0 %copy-start = (bf16[8,16,1024]{2,1,0:T(8,128)(2,1)S(1)}, bf16[8,16,1024]{2,1,0:T(8,128)(2,1)}, u32[]{:S(2)}) copy-start(bf16[8,16,1024]{2,1,0:T(8,128)(2,1)} %get-tuple-element.11) | copy-start | bytes 786436

commit v3 on v2

--- a/solution.py
+++ b/solution.py
@@ -24,7 +24,7 @@
 def kernel(
     q_ref, k_ref, v_ref, do_ref, near_ref, zonal_ref,
     att_ref, gq_ref, gk_ref, gv_ref,
-    kv, edge, corner, gath, bias, bias_z, wide, scores, probs,
+    kv, edge, corner, gath, bias, bias_z, wide, pattern, scores, probs, dscores,
     acc, side_out, side_in, lat_out, lat_in,
     z_out, z_in1, z_mid1, z_in2, z_mid2, z_in3,
     relay, relay_g, rel_s, rel_r, fwd_s, fwd_r, relg_s, relg_r, fwdg_s, fwdg_r,
@@ -253,7 +253,7 @@
 
     def build_mask(pair):
         for half in range(2):
-            head = near_ref[pair * 2 + half]
+            head = pattern[pair * 2 + half]
             allowed = jnp.where((head == 1) | centre, 1.0, 0.0).astype(F32)
             by_lane = lax.dot_general(
                 allowed, select_a, (((0,), (0,)), ((), ())), preferred_element_type=F32
@@ -328,6 +328,9 @@
             gather_z_wait(c, d).wait_recv()
         gather_c(c, core).start()
 
+    for a in range(SPAN):
+        pattern[:, a, :] = near_ref[a]
+
     def build_masks(first, last):
         @pl.loop(first, last)
         def _(pair):
@@ -364,53 +367,62 @@
     STEPS = TILES // 8
 
     def attend(c, half):
-        here = pl.ds(pl.multiple_of(half * 128, 128), 128)
+        here = slice(half * 128, half * 128 + 128)
         there = pl.ds(pl.multiple_of(c * LANES + half * 128, 128), 128)
         pair = c * 2 + half
         q_both = split_pair(q_ref[:, :, there].reshape(128, 128).astype(F32) * 0.125)
         grad = do_ref[:, :, there].reshape(128, 128).astype(F32)
         grad_both = split_pair(grad)
+        kept = dict(highest=jnp.full((8, 256), NEVER, F32), total=jnp.zeros((8, 256), F32))
 
         def tokens(i, t):
             return kv[c, i, t * 8 : t * 8 + 8, :, here].reshape(128, 128)
 
-        highest = jnp.full((8, 256), NEVER, F32)
-        for t in range(STEPS):
+        def all_tokens(i):
+            return kv[c, i, :, :, here].reshape(TILES * 16, 128)
+
+        def at(t):
+            return slice(t * 128, t * 128 + 128)
+
+        def score(t):
             s = lax.dot_general(tokens(0, t), q_both, NT, preferred_element_type=F32)
             if t < 5:
-                s = s + bias[pair, t * 128 : t * 128 + 128, :]
+                s = s + bias[pair, at(t), :]
             else:
                 z = bias_z[(t - 5) * 128 : (t - 4) * 128, :]
                 s = s + jnp.concatenate([z, z], axis=1)
-            scores[t * 128 : t * 128 + 128, :] = s
-            highest = jnp.maximum(highest, jnp.max(s.reshape(16, 8, 256), axis=0))
-        top = jnp.max(highest, axis=0, keepdims=True)
-        total = jnp.zeros((8, 256), F32)
-        for t in range(STEPS):
-            e = jnp.exp(scores[t * 128 : t * 128 + 128, :] - top)
-            scores[t * 128 : t * 128 + 128, :] = e
-            total = total + jnp.sum(e.reshape(16, 8, 256), axis=0)
-        inverse = 1.0 / jnp.sum(total, axis=0, keepdims=True)
-        out = jnp.zeros((128, 256), F32)
-        for t in range(STEPS):
-            p = scores[t * 128 : t * 128 + 128, :] * inverse
-            scores[t * 128 : t * 128 + 128, :] = p
-            p = p.astype(BF)
-            probs[t * 128 : t * 128 + 128, :] = p
-            out = out + lax.dot_general(tokens(1, t), p, TN, preferred_element_type=F32)
-        out = own_heads(out)
-        att_ref[:, :, there] = out.T.astype(BF).reshape(8, 16, 128)
-        prod = out * grad.T
-        delta = jnp.concatenate(
-            [jnp.sum(prod[0:64], axis=0, keepdims=True), jnp.sum(prod[64:128], axis=0, keepdims=True)], axis=1
-        )
-        grad_q = jnp.zeros((128, 256), F32)
-        for t in range(STEPS):
+            scores[half, at(t), :] = s
+            kept["highest"] = jnp.maximum(kept["highest"], jnp.max(s.reshape(16, 8, 256), axis=0))
+
+        def exponential(t):
+            if t == 0:
+                kept["top"] = jnp.max(kept["highest"], axis=0, keepdims=True)
+            e = jnp.exp(scores[half, at(t), :] - kept["top"])
+            scores[half, at(t), :] = e
+            kept["total"] = kept["total"] + jnp.sum(e.reshape(16, 8, 256), axis=0)
+
+        def weigh(t):
+            if t == 0:
+                kept["inverse"] = 1.0 / jnp.sum(kept["total"], axis=0, keepdims=True)
+            p = scores[half, at(t), :] * kept["inverse"]
+            scores[half, at(t), :] = p
+            probs[half, at(t), :] = p.astype(BF)
+
+        def attended():
+            out = lax.dot_general(all_tokens(1), probs[half], TN, preferred_element_type=F32)
+            out = own_heads(out)
+            att_ref[:, :, there] = out.T.astype(BF).reshape(8, 16, 128)
+            prod = out * grad.T
+            kept["delta"] = jnp.concatenate(
+                [jnp.sum(prod[0:64], axis=0, keepdims=True), jnp.sum(prod[64:128], axis=0, keepdims=True)], axis=1
+            )
+
+        def back(t):
             dp = lax.dot_general(tokens(1, t), grad_both, NT, preferred_element_type=F32)
-            ds = (scores[t * 128 : t * 128 + 128, :] * (dp - delta)).astype(BF)
-            grad_q = grad_q + lax.dot_general(tokens(0, t), ds, TN, preferred_element_type=F32)
+            ds = (scores[half, at(t), :] * (dp - kept["delta"])).astype(BF)
+            dscores[half, at(t), :] = ds
             dk = lax.dot_general(ds, q_both, NN, preferred_element_type=F32)
-            dv = lax.dot_general(probs[t * 128 : t * 128 + 128, :], grad_both, NN, preferred_element_type=F32)
+            dv = lax.dot_general(probs[half, at(t), :], grad_both, NN, preferred_element_type=F32)
             if t < 5:
                 for i, d in enumerate((dk, dv)):
                     d = d.reshape(8, 16, 128)
@@ -426,8 +438,35 @@
             else:
                 both = jnp.concatenate([dk.reshape(16, 8, 128), dv.reshape(16, 8, 128)], axis=1)
                 z_out[c, t - 5, :, :, here] = both.astype(BF)
-        grad_q = own_heads(grad_q) * 0.125
-        gq_ref[:, :, there] = grad_q.T.astype(BF).reshape(8, 16, 128)
+
+        def query_grads():
+            grad_q = lax.dot_general(all_tokens(0), dscores[half], TN, preferred_element_type=F32)
+            grad_q = own_heads(grad_q) * 0.125
+            gq_ref[:, :, there] = grad_q.T.astype(BF).reshape(8, 16, 128)
+
+        passes = [score, exponential, weigh, back]
+        steps = [[lambda t=t, f=f: f(t) for t in range(STEPS)] for f in passes]
+        steps[2].append(attended)
+        steps[3].append(query_grads)
+        return steps
+
+    def run(*lists):
+        for n in range(max(len(steps) for steps in lists)):
+            for steps in lists:
+                if n < len(steps):
+                    steps[n]()
+
+    def attend_one(c, half):
+        for steps in attend(c, half):
+            run(steps)
+
+    def attend_both(c):
+        one, two = attend(c, 0), attend(c, 1)
+        run(one[0])
+        run(one[1], two[0])
+        run(one[2], two[1])
+        run(one[3], two[2])
+        run(two[3])
 
     def load(c):
         gather_c(c, 1 - core).wait_recv()
@@ -529,12 +568,21 @@
         def _():
             relay_rows(3)
 
-        attend(c, 0)
-
         @pl.when(c < CHUNKS - 1)
         def _():
             prepare_b(c + 1)
 
+        @pl.when(c < CHUNKS - 2)
+        def _():
+            send_pooled(c + 2)
+
+        attend_both(c)
+        stage1(c)
+
+        @pl.when(c < CHUNKS - 2)
+        def _():
+            prepare_a(c + 2)
+
         @pl.when(c > 0)
         def _():
             stage2_zonal(c - 1)
@@ -543,31 +591,19 @@
         def _():
             stage3(c - 2)
 
-        @pl.when(c < CHUNKS - 2)
-        def _():
-            send_pooled(c + 2)
-            prepare_a(c + 2)
-
-        attend(c, 1)
-        stage1(c)
-
-        @pl.when(c > 0)
+        @pl.when((c > 0) & (c < CHUNKS - 1))
         def _():
             stage2_side(c - 1)
 
-        @pl.when(c > 1)
-        def _():
-            relay_grads(c - 2)
-
-        @pl.when(c > 2)
-        def _():
-            stage4(c - 3)
-
     stage2_zonal(CHUNKS - 1)
+    stage2_side(CHUNKS - 2)
+    relay_grads(0)
+    relay_grads(1)
     stage3(CHUNKS - 2)
+    stage3(CHUNKS - 1)
     stage2_side(CHUNKS - 1)
-    relay_grads(CHUNKS - 2)
-    stage3(CHUNKS - 1)
+    stage4(0)
+    relay_grads(2)
     stage4(1)
     stage4(2)
     stage4(3)
@@ -602,6 +638,11 @@
             pass_on_grads(c).wait_send()
 
     gather_y(why).wait_send()
+
+
+def hand_over(*refs):
+    for src, dst in zip(refs[:4], refs[4:]):
+        dst[...] = src[...]
 
 
 def body(queries, keys, values, cotangent, near_pattern, zonal_pattern):
@@ -616,8 +657,10 @@
         vm((8, 640, 256), F32),
         vm((SECT * 8, 128), F32),
         vm((32, 512), F32),
-        vm((TILES * 16, 256), F32),
-        vm((TILES * 16, 256), BF),
+        vm((16, SPAN, SPAN), jnp.int32),
+        vm((2, TILES * 16, 256), F32),
+        vm((2, TILES * 16, 256), BF),
+        vm((2, TILES * 16, 256), BF),
         vm((CHUNKS, 2, REGION, 16, LANES), F32),
         vm((CHUNKS, 2, 2, 10, 16, LANES), BF),
         vm((CHUNKS, 2, 2, 10, 16, LANES), BF),
@@ -635,7 +678,7 @@
     sems = [(CHUNKS, 2), (CHUNKS,), (CHUNKS,), (CHUNKS,), (CHUNKS, 4), (CHUNKS, 2), (CHUNKS, 4), (CHUNKS, ZN), (1,), (CHUNKS,), (CHUNKS, 2), (CHUNKS, 2), (CHUNKS,), (CHUNKS,), (CHUNKS, ZN)]
     for shape in sems:
         scratch += [dma(shape), dma(shape)]
-    return pl.pallas_call(
+    results = pl.pallas_call(
         kernel,
         out_shape=[block] * 4,
         in_specs=[pl.BlockSpec(memory_space=pltpu.VMEM)] * 6,
@@ -645,7 +688,14 @@
             collective_id=0, has_side_effects=True, vmem_limit_bytes=56 * 1024 * 1024
         ),
         cost_estimate=pl.CostEstimate(flops=3_000_000_000, bytes_accessed=2 << 20, transcendentals=1 << 20),
-    )(queries, keys, values, cotangent, near_pattern, zonal_pattern)
+    )(queries, keys, values, cotangent, jnp.swapaxes(near_pattern, 0, 1), zonal_pattern)
+
+    return pl.pallas_call(
+        hand_over,
+        out_shape=[block] * 4,
+        in_specs=[pl.BlockSpec(memory_space=pltpu.VMEM)] * 4,
+        out_specs=[pl.BlockSpec(memory_space=pltpu.VMEM)] * 4,
+    )(*results)
 
 
 def solution(mesh):

time: 68.6 us -> 62.5 us (0.911)
  the two profiles are of different devices: /device:TPU:24 before, /device:TPU:1 now
where the time goes in v3:
time: 62.5 us; the launch traced here: 61.6 us
  Pallas kernels  61 us (98%)
  between operations  0.64 us (1%)
    pallas_call x1, Pallas kernels, body(): pl.pallas_call(kernel, out_shape=[block] * 4, in_specs=[pl.BlockSpec(memo...  58.8 us
    pallas_call x1, Pallas kernels, body(): pl.pallas_call(hand_over, out_shape=[block] * 4, in_specs=[pl.BlockSpec(m...  2.17 us

profile of v3, /device:TPU:1, one launch (start us, length us, event | category | flops | bytes accessed | tf_op | source)
XLA Modules:
  0.0 61.6 jit_solution(10335398175209405514)
XLA Ops:
  0.6 58.8 %shard_map.93 = (bf16[8,16,1024]{2,1,0:T(8,128)(2,1)}, bf16[8,16,1024]{2,1,0:T(8,128)(2,1)}, bf16[8,16,1024]{2,1,0:T(8,128)(2,1)}, bf16[8,16,1024]{2,1,0:T(8,128)(2,1)}) custom-call(bf16[8,16,1024]{2,1,0:T(8,128)(2,1)} %q_ref.1, bf16[8,16,1024]{2,1,0:T(8,128)(2,1)} %k_ref.1, bf16[8,16,1024]{2,1,0:T(8,128)(2,1)} %v_ref.1, bf16[8,16,1024]{2,1,0:T(8,128)(2,1)} %do_ref.1, ...), custom_call_target="tpu_custom_call" | custom-call | flops 3000000000 | bytes 2097152 | tf_op jit(solution)/shard_map/pallas_call | solution.py:681
  59.5 2.2 %shard_map.94 = (bf16[8,16,1024]{2,1,0:T(8,128)(2,1)}, bf16[8,16,1024]{2,1,0:T(8,128)(2,1)}, bf16[8,16,1024]{2,1,0:T(8,128)(2,1)}, bf16[8,16,1024]{2,1,0:T(8,128)(2,1)}) custom-call(bf16[8,16,1024]{2,1,0:T(8,128)(2,1)} %get-tuple-element.8.refs_0_, bf16[8,16,1024]{2,1,0:T(8,128)(2,1)} %get-tuple-element.9.refs_1_, ...), custom_call_target="tpu_custom_call" | custom-call | tf_op jit(solution)/shard_map/pallas_call | solution.py:693

commit v4 on v3

--- a/solution.py
+++ b/solution.py
@@ -22,8 +22,9 @@
 
 
 def kernel(
-    q_ref, k_ref, v_ref, do_ref, near_ref, zonal_ref,
-    att_ref, gq_ref, gk_ref, gv_ref,
+    q_in, k_in, v_in, do_in, near_ref, zonal_ref,
+    att_out, gq_out, gk_ref, gv_ref,
+    q_ref, k_ref, v_ref, do_ref, att_ref, gq_ref, in_sem, out_sem,
     kv, edge, corner, gath, bias, bias_z, wide, pattern, scores, probs, dscores,
     acc, side_out, side_in, lat_out, lat_in,
     z_out, z_in1, z_mid1, z_in2, z_mid2, z_in3,
@@ -62,6 +63,19 @@
     @pl.when(far_up)
     def _():
         pl.semaphore_signal(barrier, inc=1, device_id=(up, y_peer), device_id_type=MESH)
+
+    loads = [
+        pltpu.make_async_copy(src, dst, in_sem.at[n])
+        for n, (src, dst) in enumerate(((k_in, k_ref), (v_in, v_ref), (q_in, q_ref), (do_in, do_ref)))
+    ]
+    for load_one in loads:
+        load_one.start()
+    for load_one in loads:
+        load_one.wait()
+    stores = [
+        pltpu.make_async_copy(src, dst, out_sem.at[n])
+        for n, (src, dst) in enumerate(((att_ref, att_out), (gq_ref, gq_out)))
+    ]
 
     def remote(src, dst, send, recv, peer):
         return pltpu.make_async_remote_copy(
@@ -596,6 +610,8 @@
             stage2_side(c - 1)
 
     stage2_zonal(CHUNKS - 1)
+    for store in stores:
+        store.start()
     stage2_side(CHUNKS - 2)
     relay_grads(0)
     relay_grads(1)
@@ -608,6 +624,9 @@
     stage4(2)
     stage4(3)
 
+    for store in stores:
+        store.wait()
+
     @pl.loop(0, CHUNKS)
     def _(c):
         below, above = lat_copies(c)
@@ -649,7 +668,7 @@
     block = jax.ShapeDtypeStruct(queries.shape, BF)
     dma = pltpu.SemaphoreType.DMA
     vm = pltpu.VMEM
-    scratch = [
+    scratch = [vm(queries.shape, BF)] * 6 + [dma((4,)), dma((2,))] + [
         vm((CHUNKS, 2, TILES, 16, LANES), BF),
         vm((CHUNKS, 2, 2, 4, 16, LANES), BF),
         vm((CHUNKS, 2, 2, 2, 3, 16, LANES), BF),
@@ -681,8 +700,8 @@
     results = pl.pallas_call(
         kernel,
         out_shape=[block] * 4,
-        in_specs=[pl.BlockSpec(memory_space=pltpu.VMEM)] * 6,
-        out_specs=[pl.BlockSpec(memory_space=pltpu.VMEM)] * 4,
+        in_specs=[pl.BlockSpec(memory_space=pl.ANY)] * 4 + [pl.BlockSpec(memory_space=pltpu.VMEM)] * 2,
+        out_specs=[pl.BlockSpec(memory_space=pl.ANY)] * 2 + [pl.BlockSpec(memory_space=pltpu.VMEM)] * 2,
         scratch_shapes=scratch,
         compiler_params=pltpu.CompilerParams(
             collective_id=0, has_side_effects=True, vmem_limit_bytes=56 * 1024 * 1024

time: 62.5 us -> 62.1 us (level)
  no operation moved by 1% of the time
where the time goes in v4:
time: 62.1 us; the launch traced here: 61.2 us
  Pallas kernels  60.5 us (97%)
  between operations  0.64 us (1%)
    pallas_call x1, Pallas kernels, body(): pl.pallas_call(kernel, out_shape=[block] * 4, in_specs=[pl.BlockSpec(memo...  58.4 us
    pallas_call x1, Pallas kernels, body(): pl.pallas_call(hand_over, out_shape=[block] * 4, in_specs=[pl.BlockSpec(m...  2.17 us

profile of v4, /device:TPU:1, one launch (start us, length us, event | category | flops | bytes accessed | tf_op | source)
XLA Modules:
  0.0 61.2 jit_solution(16794528499072388004)
XLA Ops:
  0.6 58.4 %shard_map.93 = (bf16[8,16,1024]{2,1,0:T(8,128)(2,1)}, bf16[8,16,1024]{2,1,0:T(8,128)(2,1)}, bf16[8,16,1024]{2,1,0:T(8,128)(2,1)}, bf16[8,16,1024]{2,1,0:T(8,128)(2,1)}) custom-call(bf16[8,16,1024]{2,1,0:T(8,128)(2,1)} %q_in.1, bf16[8,16,1024]{2,1,0:T(8,128)(2,1)} %k_in.1, bf16[8,16,1024]{2,1,0:T(8,128)(2,1)} %v_in.1, bf16[8,16,1024]{2,1,0:T(8,128)(2,1)} %do_in.1, ...), custom_call_target="tpu_custom_call" | custom-call | flops 3000000000 | bytes 2097152 | tf_op jit(solution)/shard_map/pallas_call | solution.py:700
  59.0 2.2 %shard_map.94 = (bf16[8,16,1024]{2,1,0:T(8,128)(2,1)}, bf16[8,16,1024]{2,1,0:T(8,128)(2,1)}, bf16[8,16,1024]{2,1,0:T(8,128)(2,1)}, bf16[8,16,1024]{2,1,0:T(8,128)(2,1)}) custom-call(bf16[8,16,1024]{2,1,0:T(8,128)(2,1)} %get-tuple-element.8.refs_0_, bf16[8,16,1024]{2,1,0:T(8,128)(2,1)} %get-tuple-element.9.refs_1_, ...), custom_call_target="tpu_custom_call" | custom-call | tf_op jit(solution)/shard_map/pallas_call | solution.py:712
